TPU v7x, 256 devices: a whole 4x4x8 slice. The times are simulated.
256 devices in a mesh: rve: 32 (over x, z), slab: 8 (over y, core).
Axes of the slice: x: 4, y: 4, z: 8, core: 2. Of those that a mesh axis runs over, the one named last changes fastest.
Arguments:
- displacement: float32 [2, 8192, 128], P(None, ('rve', 'slab'))
- body_force: float32 [2, 8192, 128], P(None, ('rve', 'slab')), may hold values from -6 to 6
- assignment: int32 [4, 8192, 128], P(None, ('rve', 'slab')), may hold values from 0 to 31, as said below
- phases: int32 [32, 256, 256], P('rve', 'slab'), may hold values from 0 to 1
- flags: int32 [32, 256, 256], P('rve', 'slab'), may hold values 0 or 1
Outputs:
- correction: float32 [2, 8192, 128], P(None, ('rve', 'slab'))
- micro_strain: float32 [32, 3, 256, 256], P('rve', None, 'slab')
- homogenised: float32 [12, 32], replicated
Inputs may be any that keep to these rules, and one draw needn't show every extreme that they name: `assignment`: every one of the 32 RVEs is named by at least one point.
All inputs are finite; a program needn't handle non-finite values. No bound on the sum of `flags` on one device may be relied on, other than what follows from the above.
Results may differ from a plain program's by a relative error of at most 0.0003.
Values sent between devices are 32-bit elements; how exact they have to be, the bound alone decides.
A program may use at most 64 MiB of HBM per device.

v0:
```python
import math

import jax
import jax.numpy as jnp
from jax import lax
from jax.sharding import PartitionSpec as P

ITERS = 2
CG_STEPS = 4


MU_REF = 2.0
LAMBDA_REF = 2.0
COUPLE = (LAMBDA_REF + MU_REF) / (MU_REF * (LAMBDA_REF + 2.0 * MU_REF))
LOWER = 0.5 - 0.5 / math.sqrt(3.0)
UPPER = 0.5 + 0.5 / math.sqrt(3.0)
POINTS = ((LOWER, LOWER), (UPPER, LOWER), (LOWER, UPPER), (UPPER, UPPER))
WEIGHT = 0.25
HIGHEST = lax.Precision.HIGHEST


def passed_along(value, axis, steps):
    count = lax.axis_size(axis)
    leading, last = (max(0, -steps), min(count, count - steps))
    return lax.ppermute(value, axis, [(source, source + steps) for source in range(leading, last)])


def shape_slopes(point):
    coord_s, coord_t = point
    along_x = (-(1.0 - coord_t), 1.0 - coord_t, -coord_t, coord_t)
    along_y = (-(1.0 - coord_s), -coord_s, 1.0 - coord_s, coord_s)
    return (along_x, along_y)


def rows_up(field):
    return jnp.concatenate([field[..., 1:], jnp.zeros_like(field[..., :1])], -1)


def rows_down(field):
    return jnp.concatenate([jnp.zeros_like(field[..., :1]), field[..., :-1]], -1)


def corner_fields(field):
    edge = passed_along(field[:, :1, :], ("rve", "slab"), -1)
    right = jnp.concatenate([field[:, 1:], edge], 1)
    return (field, right, rows_up(field), rows_up(right))


def strains_at(corners, point):
    along_x, along_y = shape_slopes(point)
    first = sum((along_x[a] * corners[a][0] for a in range(4)))
    second = sum((along_y[a] * corners[a][1] for a in range(4)))
    shear = sum((along_y[a] * corners[a][0] + along_x[a] * corners[a][1] for a in range(4)))
    return jnp.stack([first, second, shear])


def nodal_terms(stress, point):
    along_x, along_y = shape_slopes(point)
    terms = []
    for a in range(4):
        force_x = WEIGHT * (along_x[a] * stress[0] + along_y[a] * stress[2])
        force_y = WEIGHT * (along_y[a] * stress[1] + along_x[a] * stress[2])
        terms.append(jnp.stack([force_x, force_y]))
    return terms


def assemble(terms):
    gathered = terms[1] + rows_down(terms[3])
    incoming = passed_along(gathered[:, -1:, :], ("rve", "slab"), 1)
    shifted = jnp.concatenate([incoming, gathered[:, :-1]], 1)
    return terms[0] + rows_down(terms[2]) + shifted


def contract(tangent, vector):
    return jnp.stack(
        [
            tangent[c] * vector[0] + tangent[3 + c] * vector[1] + tangent[6 + c] * vector[2]
            for c in range(3)
        ]
    )


def inner_product(left, right):
    return lax.psum(jnp.sum(left * right), ("rve", "slab"))


def material(strain, bulk, shear, harden):
    volume = strain[0, 0] + strain[0, 1]
    normal_dev = 0.5 * (strain[0, 0] - strain[0, 1])
    shear_half = 0.5 * strain[0, 2]
    radius = 2.0 * normal_dev * normal_dev + 2.0 * shear_half * shear_half
    stiff = harden * radius
    factor = jnp.ones_like(radius)
    for turn in range(3):
        factor = factor - (factor + stiff * factor * factor * factor - 1.0) / (
            1.0 + 3.0 * stiff * factor * factor
        )
    slope = -harden * factor * factor * factor / (1.0 + 3.0 * stiff * factor * factor)
    stress = jnp.stack(
        [
            bulk * volume + 2.0 * shear * factor * normal_dev,
            bulk * volume - 2.0 * shear * factor * normal_dev,
            2.0 * shear * factor * shear_half,
        ]
    )
    rest = strain[1:]
    d_volume = rest[:, 0] + rest[:, 1]
    d_normal = 0.5 * (rest[:, 0] - rest[:, 1])
    d_shear = 0.5 * rest[:, 2]
    d_factor = slope * (4.0 * normal_dev * d_normal + 4.0 * shear_half * d_shear)
    d_dev = 2.0 * shear * (factor * d_normal + d_factor * normal_dev)
    images = jnp.stack(
        [
            bulk * d_volume + d_dev,
            bulk * d_volume - d_dev,
            2.0 * shear * (factor * d_shear + d_factor * shear_half),
        ],
        1,
    )
    return jnp.concatenate([stress[None], images], 0)


def frequencies(size):
    index = jnp.arange(size, dtype=jnp.int32)
    wrapped = jnp.where(index == size // 2, 0, index - size)
    return jnp.where(index < size // 2, index, wrapped).astype(jnp.float32)


def wave_tables(size):
    index = jnp.arange(size, dtype=jnp.int32)
    turns = index[:, None] * index[None, :] % size
    angle = turns.astype(jnp.float32) * (2.0 * math.pi / size)
    return (jnp.cos(angle), jnp.sin(angle))


def green_parts(freq_rows, freq_cols):
    square = freq_rows * freq_rows + freq_cols * freq_cols
    inverse = jnp.where(square > 0.0, 1.0 / jnp.maximum(square, 1.0), 0.0)
    return (
        freq_rows * freq_rows * inverse,
        freq_cols * freq_cols * inverse,
        freq_rows * freq_cols * inverse,
    )


def green(first, second, mixed, part_11, part_22, part_12):
    total = part_11 * first + 2.0 * part_12 * mixed + part_22 * second
    out_11 = (part_11 * first + part_12 * mixed) / MU_REF - COUPLE * part_11 * total
    out_22 = (part_12 * mixed + part_22 * second) / MU_REF - COUPLE * part_22 * total
    out_12 = (
        part_12 * (first + second) + (part_11 + part_22) * mixed
    ) / MU_REF - 2.0 * COUPLE * part_12 * total
    return jnp.stack([out_11, out_22, out_12], 1)


def shards(displacement, body_force, assignment, phases, flags):
    grid = phases.shape[2]
    block = phases.shape[1]
    groups = lax.axis_size("rve")
    rve_index = lax.axis_index("rve")
    slab_index = lax.axis_index("slab")
    columns = displacement.shape[1] * displacement.shape[2]
    labels = jnp.arange(groups, dtype=jnp.int32)
    corners = corner_fields(displacement)
    strains = [strains_at(corners, point) for point in POINTS]
    sums = jnp.zeros((3, groups), jnp.float32)
    counts = jnp.zeros((groups,), jnp.float32)
    for index in range(4):
        member = (assignment[index].reshape(columns, 1) == labels[None, :]).astype(jnp.float32)
        sums = sums + jnp.dot(strains[index].reshape(3, columns), member, precision=HIGHEST)
        counts = counts + jnp.sum(member, axis=0)
    sums, counts = lax.psum((sums, counts), ("rve", "slab"))
    means = sums / counts[None, :]
    own_mean = lax.dynamic_slice_in_dim(means, rve_index, 1, 1)[:, 0]
    phase = phases[0]
    flag = flags[0]
    bulk = jnp.where(phase == 1, 6.0, 2.0).astype(jnp.float32)
    shear = jnp.where(phase == 1, 3.0, 1.0).astype(jnp.float32)
    harden = flag.astype(jnp.float32) * jnp.where(phase == 1, 0.5, 2.0).astype(jnp.float32)
    cos_table, sin_table = wave_tables(grid)
    freq_cols = lax.dynamic_slice_in_dim(frequencies(grid), slab_index * block, block)
    part_11, part_22, part_12 = green_parts(frequencies(grid)[:, None], freq_cols[None, :])
    start = jnp.concatenate([own_mean[None], jnp.eye(3, dtype=jnp.float32)], 0)
    strain = jnp.broadcast_to(start[:, :, None, None], (4, 3, block, grid))
    for step in range(ITERS):
        stress = material(strain, bulk, shear, harden)
        spec_real = jnp.einsum("ncxy,yk->ncxk", stress, cos_table, precision=HIGHEST)
        spec_imag = -jnp.einsum("ncxy,yk->ncxk", stress, sin_table, precision=HIGHEST)
        spectrum = jnp.stack([spec_real, spec_imag], 1)
        items = lax.all_to_all(spectrum, "slab", split_axis=4, concat_axis=3, tiled=True)
        real_part = items[:, 0]
        imag_part = items[:, 1]
        filter_spec_real = jnp.einsum(
            "kx,ncxy->ncky", cos_table, real_part, precision=HIGHEST
        ) + jnp.einsum("kx,ncxy->ncky", sin_table, imag_part, precision=HIGHEST)
        filter_spec_imag = jnp.einsum(
            "kx,ncxy->ncky", cos_table, imag_part, precision=HIGHEST
        ) - jnp.einsum("kx,ncxy->ncky", sin_table, real_part, precision=HIGHEST)
        filt_real = green(
            filter_spec_real[:, 0],
            filter_spec_real[:, 1],
            filter_spec_real[:, 2],
            part_11,
            part_22,
            part_12,
        )
        filt_imag = green(
            filter_spec_imag[:, 0],
            filter_spec_imag[:, 1],
            filter_spec_imag[:, 2],
            part_11,
            part_22,
            part_12,
        )
        back_real = jnp.einsum(
            "kx,ncxy->ncky", cos_table, filt_real, precision=HIGHEST
        ) - jnp.einsum("kx,ncxy->ncky", sin_table, filt_imag, precision=HIGHEST)
        back_imag = jnp.einsum(
            "kx,ncxy->ncky", cos_table, filt_imag, precision=HIGHEST
        ) + jnp.einsum("kx,ncxy->ncky", sin_table, filt_real, precision=HIGHEST)
        filtered = lax.all_to_all(
            jnp.stack([back_real, back_imag], 1), "slab", split_axis=3, concat_axis=4, tiled=True
        )
        out_real = jnp.einsum(
            "ncxk,ky->ncxy", filtered[:, 0], cos_table, precision=HIGHEST
        ) - jnp.einsum("ncxk,ky->ncxy", filtered[:, 1], sin_table, precision=HIGHEST)
        update = out_real / (grid * grid)
        strain = strain - update
    stress = material(strain, bulk, shear, harden)
    local = jnp.sum(stress, axis=(2, 3)).reshape(12)
    group = lax.psum(local, "slab")
    totals = lax.all_gather(group[:, None], "rve", axis=1, tiled=True)
    homogenised = totals / (grid * grid)
    table = jnp.concatenate([homogenised, means], 0)
    forces = [jnp.zeros_like(displacement) for a in range(4)]
    for index, point in enumerate(POINTS):
        looked = jnp.take(table, assignment[index], axis=1)
        point_stress = looked[0:3] + contract(looked[3:12], strains[index] - looked[12:15])
        terms = nodal_terms(point_stress, point)
        forces = [forces[a] + terms[a] for a in range(4)]
    residual = body_force - assemble(forces)

    def stiffness(field):
        beside_all = corner_fields(field)
        parts = [jnp.zeros_like(field) for a in range(4)]
        for index, point in enumerate(POINTS):
            tangent = jnp.take(homogenised[3:12], assignment[index], axis=1)
            terms = nodal_terms(contract(tangent, strains_at(beside_all, point)), point)
            parts = [parts[a] + terms[a] for a in range(4)]
        return assemble(parts)

    correction = jnp.zeros_like(residual)
    direction = residual
    rho = inner_product(residual, residual)
    for step in range(CG_STEPS):
        image = stiffness(direction)
        alpha = rho / inner_product(direction, image)
        correction = correction + alpha * direction
        residual = residual - alpha * image
        fresh = inner_product(residual, residual)
        direction = residual + fresh / rho * direction
        rho = fresh
    return (correction, strain[0][None], homogenised)


def solution(mesh):
    return jax.shard_map(
        shards,
        mesh=mesh,
        in_specs=(
            P(None, ("rve", "slab"), None),
            P(None, ("rve", "slab"), None),
            P(None, ("rve", "slab"), None),
            P("rve", "slab", None),
            P("rve", "slab", None),
        ),
        out_specs=(P(None, ("rve", "slab"), None), P("rve", None, "slab", None), P()),
        check_vma=False,
    )
```

profile of v0, /device:TPU:1, one launch (start us, length us, event | category | flops | bytes accessed | tf_op | source)
XLA Modules:
  0.0 1029.2 jit_solution(6249196018656097657)
XLA Ops:
  1.4 5.1 collective-permute-start
  13.6 81.2 %all-reduce.21 = (f32[3,32]{1,0:T(4,128)S(1)}, f32[32]{0:T(128)S(1)}) all-reduce(f32[3,32]{1,0:T(4,128)S(1)} %convolution_add_fusion.4, f32[32]{0:T(128)S(1)} %add_add_fusion.44), channel_id=1, replica_groups=mesh['rve'=32,'slab'=8] {'rve','slab'}, use_global_device_ids=true, to_apply=%region_0.0 | all-reduce | flops 128 | bytes 1024 | tf_op jit(solution)/shard_map/psum | solution.py:172
  116.1 12.0 %all-to-all-done = f32[8,1,24576]{2,1,0:T(1,128)S(1)} async-done(((f32[8,1,24576]{2,1,0:T(1,128)}), f32[8,1,24576]{2,1,0:T(1,128)S(1)}, u32[]{:S(2)}, u32[]{:S(2)}) %all-to-all-start) | async-done | bytes 786464 | tf_op jit(solution)/shard_map/all_to_all | solution.py:190
  164.5 12.1 %all-to-all-done.1 = f32[8,1,24576]{2,1,0:T(1,128)S(1)} async-done(((f32[8,1,24576]{2,1,0:T(1,128)}), f32[8,1,24576]{2,1,0:T(1,128)S(1)}, u32[]{:S(2)}, u32[]{:S(2)}) %all-to-all-start.1) | async-done | bytes 786464 | tf_op jit(solution)/shard_map/all_to_all | solution.py:221
  202.3 16.7 %all_to_all.72 = f32[8,1,24576]{2,1,0:T(1,128)S(1)} all-to-all(f32[8,1,24576]{2,1,0:T(1,128)} %reshape.975), channel_id=1, replica_groups=mesh['rve'=32,'slab'=8] {'slab'}, dimensions={0} | all-to-all | bytes 1572864 | tf_op jit(solution)/shard_map/all_to_all | solution.py:190
  258.1 9.5 all-to-all-done.3
  283.4 12.6 %psum.79 = f32[12,1]{0,1:T(1,128)S(1)} all-reduce(f32[12,1]{0,1:T(1,128)S(1)} %broadcast_in_dim.84), channel_id=1, replica_groups=mesh['rve'=32,'slab'=8] {'slab'}, use_global_device_ids=true, to_apply=%region_7.8 | all-reduce | flops 12 | bytes 96 | tf_op jit(solution)/shard_map/psum | solution.py:231
  296.0 27.9 %all-gather = f32[32,1,12]{2,1,0:T(1,128)S(1)} all-gather(f32[1,1,12]{2,1,0:T(1,128)S(1)} %bitcast.378), channel_id=1, replica_groups=mesh['rve'=32,'slab'=8] {'rve'}, dimensions={0}, use_global_device_ids=true | all-gather | bytes 1584 | tf_op jit(solution)/shard_map/all_gather | solution.py:232
  324.1 10.9 %gather_fusion.3 = f32[4096,15]{1,0:T(8,128)S(1)} fusion(f32[15,32]{0,1:T(8,128)S(1)} %pad_maximum_fusion.89, s32[4096]{0:T(1024)S(1)} %copy-done.25), kind=kCustom, calls=%fused_computation.4.clone | custom fusion | bytes 507904 | tf_op jit(solution)/shard_map/jit(_take)/gather | solution.py:237
  335.7 10.8 %gather_fusion.2 = f32[4096,15]{1,0:T(8,128)S(1)} fusion(f32[15,32]{0,1:T(8,128)S(1)} %pad_maximum_fusion.89, s32[4096]{0:T(1024)S(1)} %copy-done.26), kind=kCustom, calls=%fused_computation.3.clone | custom fusion | bytes 507904 | tf_op jit(solution)/shard_map/jit(_take)/gather | solution.py:237
  347.1 10.8 %gather_fusion.1 = f32[4096,15]{1,0:T(8,128)S(1)} fusion(f32[15,32]{0,1:T(8,128)S(1)} %pad_maximum_fusion.89, s32[4096]{0:T(1024)S(1)} %copy-done.28), kind=kCustom, calls=%fused_computation.2.clone | custom fusion | bytes 507904 | tf_op jit(solution)/shard_map/jit(_take)/gather | solution.py:237
  358.6 10.8 %gather_fusion = f32[4096,15]{1,0:T(8,128)S(1)} fusion(f32[15,32]{0,1:T(8,128)S(1)} %pad_maximum_fusion.89, s32[4096]{0:T(1024)S(1)} %copy-done.27), kind=kCustom, calls=%fused_computation.clone | custom fusion | bytes 507904 | tf_op jit(solution)/shard_map/jit(_take)/gather | solution.py:237
  374.3 14.1 %gather_fusion.5 = f32[4096,9]{1,0:T(8,128)} fusion(f32[9,32]{0,1:T(8,128)S(1)} %slice.1619, s32[4096]{0:T(1024)S(1)} %copy-done.29), kind=kCustom, calls=%fused_computation.5.clone | custom fusion | bytes 311296 | tf_op jit(solution)/shard_map/jit(_take)/gather | solution.py:247
  388.3 14.1 %gather_fusion.4 = f32[4096,9]{1,0:T(8,128)} fusion(f32[9,32]{0,1:T(8,128)S(1)} %slice.1619, s32[4096]{0:T(1024)S(1)} %copy-done.27), kind=kCustom, calls=%fused_computation.1.clone | custom fusion | bytes 311296 | tf_op jit(solution)/shard_map/jit(_take)/gather | solution.py:247
  402.4 10.8 %gather_fusion.6 = f32[4096,9]{1,0:T(8,128)S(1)} fusion(f32[9,32]{0,1:T(8,128)S(1)} %slice.1619, s32[4096]{0:T(1024)S(1)} %copy-done.26), kind=kCustom, calls=%fused_computation.6.clone | custom fusion | bytes 311296 | tf_op jit(solution)/shard_map/jit(_take)/gather | solution.py:247
  413.2 9.8 collective-permute-start.1
  428.2 10.8 %gather_fusion.7 = f32[4096,9]{1,0:T(8,128)S(1)} fusion(f32[9,32]{0,1:T(8,128)S(1)} %slice.1619, s32[4096]{0:T(1024)S(1)} %copy-done.25), kind=kCustom, calls=%fused_computation.7.clone | custom fusion | bytes 311296 | tf_op jit(solution)/shard_map/jit(_take)/gather | solution.py:247
  448.9 83.0 %all-reduce.20 = (f32[]{:T(128)}, f32[]{:T(128)}) all-reduce(f32[]{:T(128)} %get-tuple-element.21, f32[]{:T(128)} %get-tuple-element.20), channel_id=1, replica_groups=mesh['rve'=32,'slab'=8] {'rve','slab'}, use_global_device_ids=true, to_apply=%region_9.11 | all-reduce | flops 2 | bytes 16 | tf_op jit(solution)/shard_map/psum | solution.py:84
  533.8 74.1 %psum.82 = f32[]{:T(128)} all-reduce(f32[]{:T(128)} %multiply_reduce_fusion.4), channel_id=1, replica_groups=mesh['rve'=32,'slab'=8] {'rve','slab'}, use_global_device_ids=true, to_apply=%region_13.16 | all-reduce | flops 1 | bytes 8 | tf_op jit(solution)/shard_map/psum | solution.py:84
  618.4 78.8 %psum.83 = f32[]{:T(128)} all-reduce(f32[]{:T(128)} %get-tuple-element.90), channel_id=1, replica_groups=mesh['rve'=32,'slab'=8] {'rve','slab'}, use_global_device_ids=true, to_apply=%region_15.18 | all-reduce | flops 1 | bytes 8 | tf_op jit(solution)/shard_map/psum | solution.py:84
  699.2 73.3 %psum.84 = f32[]{:T(128)} all-reduce(f32[]{:T(128)} %get-tuple-element.88), channel_id=1, replica_groups=mesh['rve'=32,'slab'=8] {'rve','slab'}, use_global_device_ids=true, to_apply=%region_17.20 | all-reduce | flops 1 | bytes 8 | tf_op jit(solution)/shard_map/psum | solution.py:84
  783.0 78.8 %psum.85 = f32[]{:T(128)} all-reduce(f32[]{:T(128)} %get-tuple-element.56), channel_id=1, replica_groups=mesh['rve'=32,'slab'=8] {'rve','slab'}, use_global_device_ids=true, to_apply=%region_19.22 | all-reduce | flops 1 | bytes 8 | tf_op jit(solution)/shard_map/psum | solution.py:84
  863.8 73.3 %psum.86 = f32[]{:T(128)} all-reduce(f32[]{:T(128)} %multiply_reduce_fusion), channel_id=1, replica_groups=mesh['rve'=32,'slab'=8] {'rve','slab'}, use_global_device_ids=true, to_apply=%region_21.24 | all-reduce | flops 1 | bytes 8 | tf_op jit(solution)/shard_map/psum | solution.py:84
  948.3 78.7 %psum.87 = f32[]{:T(128)} all-reduce(f32[]{:T(128)} %fusion.228), channel_id=1, replica_groups=mesh['rve'=32,'slab'=8] {'rve','slab'}, use_global_device_ids=true, to_apply=%region_23.26 | all-reduce | flops 1 | bytes 8 | tf_op jit(solution)/shard_map/psum | solution.py:84
  (344 shorter events, 193.2 us)
Async XLA Ops:
  0.6 100.2 %copy-start.43 = (s32[1,32,256]{2,1,0:T(8,128)S(1)}, s32[1,32,256]{2,1,0:T(8,128)}, u32[]{:S(2)}) copy-start(s32[1,32,256]{2,1,0:T(8,128)} %param.12) | copy-start | bytes 98308
  0.6 100.2 %copy-start = (s32[1,32,256]{2,1,0:T(8,128)S(1)}, s32[1,32,256]{2,1,0:T(8,128)}, u32[]{:S(2)}) copy-start(s32[1,32,256]{2,1,0:T(8,128)} %param.13) | copy-start | bytes 98308
  1.4 8.1 collective-permute-start
  111.4 16.6 %all-to-all-start = ((f32[8,1,24576]{2,1,0:T(1,128)}), f32[8,1,24576]{2,1,0:T(1,128)S(1)}, u32[]{:S(2)}, u32[]{:S(2)}) async-start(f32[8,1,24576]{2,1,0:T(1,128)} %reshape.971), calls=%async_computation | async-start | bytes 1572864 | tf_op jit(solution)/shard_map/all_to_all | solution.py:190
  116.0 30.9 %copy-start.19 = (f32[256,32]{0,1:T(8,128)}, f32[256,32]{0,1:T(8,128)S(1)}, u32[]{:S(2)}) copy-start(f32[256,32]{0,1:T(8,128)S(1)} %get-tuple-element.438) | copy-start | bytes 98308
  116.0 30.9 %copy-start.21 = (f32[256,32]{0,1:T(8,128)}, f32[256,32]{0,1:T(8,128)S(1)}, u32[]{:S(2)}) copy-start(f32[256,32]{0,1:T(8,128)S(1)} %get-tuple-element.446) | copy-start | bytes 98308
  116.0 30.9 %copy-start.23 = (f32[256,32]{0,1:T(8,128)}, f32[256,32]{0,1:T(8,128)S(1)}, u32[]{:S(2)}) copy-start(f32[256,32]{0,1:T(8,128)S(1)} %get-tuple-element.448) | copy-start | bytes 98308
  116.0 31.0 %copy-start.6 = (f32[256,32]{0,1:T(8,128)}, f32[256,32]{0,1:T(8,128)S(1)}, u32[]{:S(2)}) copy-start(f32[256,32]{0,1:T(8,128)S(1)} %get-tuple-element.439) | copy-start | bytes 98308
  116.0 31.0 %copy-start.8 = (f32[256,32]{0,1:T(8,128)}, f32[256,32]{0,1:T(8,128)S(1)}, u32[]{:S(2)}) copy-start(f32[256,32]{0,1:T(8,128)S(1)} %get-tuple-element.447) | copy-start | bytes 98308
  116.0 31.0 %copy-start.13 = (f32[256,32]{0,1:T(8,128)}, f32[256,32]{0,1:T(8,128)S(1)}, u32[]{:S(2)}) copy-start(f32[256,32]{0,1:T(8,128)S(1)} %get-tuple-element.437) | copy-start | bytes 98308
  116.0 31.0 %copy-start.15 = (f32[256,32]{0,1:T(8,128)}, f32[256,32]{0,1:T(8,128)S(1)}, u32[]{:S(2)}) copy-start(f32[256,32]{0,1:T(8,128)S(1)} %get-tuple-element.444) | copy-start | bytes 98308
  116.0 31.0 %copy-start.17 = (f32[256,32]{0,1:T(8,128)}, f32[256,32]{0,1:T(8,128)S(1)}, u32[]{:S(2)}) copy-start(f32[256,32]{0,1:T(8,128)S(1)} %get-tuple-element.445) | copy-start | bytes 98308
  160.1 16.6 %all-to-all-start.1 = ((f32[8,1,24576]{2,1,0:T(1,128)}), f32[8,1,24576]{2,1,0:T(1,128)S(1)}, u32[]{:S(2)}, u32[]{:S(2)}) async-start(f32[8,1,24576]{2,1,0:T(1,128)} %reshape.973), calls=%async_computation.1 | async-start | bytes 1572864 | tf_op jit(solution)/shard_map/all_to_all | solution.py:221
  250.8 16.8 %all-to-all-start.3 = ((f32[8,1,24576]{2,1,0:T(1,128)}), f32[8,1,24576]{2,1,0:T(1,128)S(1)}, u32[]{:S(2)}, u32[]{:S(2)}) async-start(f32[8,1,24576]{2,1,0:T(1,128)} %reshape.977), calls=%async_computation.3 | async-start | bytes 1572864 | tf_op jit(solution)/shard_map/all_to_all | solution.py:221
  281.3 42.8 %copy-start.25 = (s32[4096]{0:T(1024)S(1)}, s32[4096]{0:T(1024)}, u32[]{:S(2)}) copy-start(s32[4096]{0:T(1024)} %get-tuple-element.231) | copy-start | bytes 49156
  413.2 26.4 %collective-permute-start.1 = (f32[2,1,128]{2,1,0:T(1,128)S(1)}, f32[2,1,128]{2,1,0:T(1,128)S(1)}, u32[]{:S(2)}, u32[]{:S(2)}) collective-permute-start(f32[2,1,128]{2,1,0:T(1,128)S(1)} %pad_add_fusion.9), channel_id=1, source_target_pairs={{0,1},{1,2},{2,3},{3,4},{4,5},{5,6},{6,7},{7,8},{8,9},{9,10},{10,1... | collective-permute-start | bytes 3080 | tf_op jit(solution)/shard_map/ppermute | solution.py:25
  439.7 4.9 collective-permute-start.2
  445.2 3.0 collective-permute-start.3
  609.3 4.9 collective-permute-start.4
  614.7 3.0 collective-permute-start.5
  773.8 4.9 collective-permute-start.6
  779.3 3.0 collective-permute-start.7
  938.5 4.9 collective-permute-start.8
  944.0 3.0 collective-permute-start.9
  (35 other events, 170.7 us)
where the time goes:
time: 1040 us; the launch traced here: 1030 us
  blocking collectives  678 us (65%)
  local copies, waits for them, and re-layouts  167 us (16%)
  starting transfers between devices  46.7 us (4%)
  waiting for transfers between devices  45.4 us (4%)
  other arithmetic  38 us (4%)
  matrix products  37.4 us (4%)
  between operations  16.2 us (2%)
    psum x7, blocking collectives, inner_product(): return lax.psum(jnp.sum(left * right), ('rve', 'slab'))  540 us
    psum x1, blocking collectives, shards(): sums, counts = lax.psum((sums, counts), ('rve', 'slab'))  81.2 us
    gather x8, local copies, waits for them, and re-layouts, stiffness(): tangent = jnp.take(homogenised[3:12], assignment[index], axis=1)  55.4 us
    gather x8, local copies, waits for them, and re-layouts, shards(): looked = jnp.take(table, assignment[index], axis=1)  45.8 us
    ppermute x10, starting transfers between devices, passed_along(): lax.ppermute(value, axis, [(source, source + steps) for source in range(l...  33.5 us
    all_gather x1, blocking collectives, shards(): totals = lax.all_gather(group[:, None], 'rve', axis=1, tiled=True)  27.9 us
    unnamed x101, local copies, waits for them, and re-layouts  23.8 us
    all_to_all x2, waiting for transfers between devices, shards(): lax.all_to_all(jnp.stack([back_real, back_imag], 1), 'slab', split_axis=3...  21.6 us
  transfers between devices with their start and end apart: 13, of which 11 were waited for; matrix products, arithmetic and copies ran while one was open for 2% of the time, Pallas kernels for 0%

commit v1 on v0

v1 whole, which is shorter than its diff:
```python
import math

import jax
import jax.numpy as jnp
import ml_dtypes
import numpy as np
from jax import lax
from jax.experimental import pallas as pl
from jax.experimental.pallas import tpu as pltpu
from jax.sharding import PartitionSpec as P

MESH = pl.DeviceIdType.MESH
F32 = jnp.float32
BF16 = jnp.bfloat16

GRID = 256
HALF = 128
GROUPS = 32
SLABS = 8
BLOCK = 32
EXT = 48
CG_STEPS = 4

MU_REF = 2.0
LAMBDA_REF = 2.0
COUPLE = (LAMBDA_REF + MU_REF) / (MU_REF * (LAMBDA_REF + 2.0 * MU_REF))
LOWER = 0.5 - 0.5 / math.sqrt(3.0)
UPPER = 0.5 + 0.5 / math.sqrt(3.0)
ENDS = (LOWER, UPPER)
WEIGHT = 0.25
RANGE = 0.5

PAIRS = [(i, j) for i in range(CG_STEPS) for j in range(i, CG_STEPS + 1)]


def transform_tables():
    n = GRID
    place = np.arange(n)
    rows = []
    for slot in range(n):
        if slot < HALF:
            scale = math.sqrt((1.0 if slot == 0 else 2.0) / n)
            rows.append(scale * np.cos(2.0 * np.pi * (slot * place % n) / n))
        elif slot == HALF:
            rows.append(math.sqrt(1.0 / n) * np.cos(np.pi * place))
        else:
            rows.append(math.sqrt(2.0 / n) * np.sin(2.0 * np.pi * ((slot - HALF) * place % n) / n))
    forward = np.stack(rows).astype(np.float32)
    tables = []
    for table in (forward, forward.T):
        high = table.astype(ml_dtypes.bfloat16)
        low = (table - high.astype(np.float32)).astype(ml_dtypes.bfloat16)
        tables += [high, low]
    return np.stack(tables)


def lane_iota(shape):
    return lax.broadcasted_iota(jnp.int32, shape, len(shape) - 1)


def rows_up(field):
    rolled = pltpu.roll(field, field.shape[1] - 1, 1)
    return jnp.where(lane_iota(field.shape) == field.shape[1] - 1, 0.0, rolled)


def rows_down(field):
    rolled = pltpu.roll(field, 1, 1)
    return jnp.where(lane_iota(field.shape) == 0, 0.0, rolled)


def columns_back(field):
    return pltpu.roll(field, field.shape[0] - 1, 0)


def columns_on(field):
    return pltpu.roll(field, 1, 0)


def split(value):
    high = value.astype(BF16)
    return high, (value - high.astype(F32)).astype(BF16)


def dot(left, right):
    return jnp.dot(left, right, preferred_element_type=F32)


def strain_parts(first, second, first_next, second_next):
    across_1 = first_next - first
    across_2 = second_next - second
    across_1_up, across_2_up = rows_up(across_1), rows_up(across_2)
    up_1, up_2 = rows_up(first) - first, rows_up(second) - second
    up_1_next = rows_up(first_next) - first_next
    up_2_next = rows_up(second_next) - second_next
    d1x = [(1.0 - t) * across_1 + t * across_1_up for t in ENDS]
    d2x = [(1.0 - t) * across_2 + t * across_2_up for t in ENDS]
    d1y = [(1.0 - s) * up_1 + s * up_1_next for s in ENDS]
    d2y = [(1.0 - s) * up_2 + s * up_2_next for s in ENDS]
    return d1x, d2y, d1y, d2x


def assemble(stress):
    by_t = lambda c, t: stress[2 * t][c] + stress[2 * t + 1][c]
    by_s = lambda c, s: stress[s][c] + stress[2 + s][c]

    def mixed(parts):
        low = sum(WEIGHT * (1.0 - ENDS[k]) * parts[k] for k in range(2))
        high = sum(WEIGHT * ENDS[k] * parts[k] for k in range(2))
        return low, high

    forces = []
    for normal_x, normal_y in ((0, 2), (2, 1)):
        low, high = mixed([by_t(normal_x, t) for t in range(2)])
        over_x = low + rows_down(high)
        low, high = mixed([by_s(normal_y, s) for s in range(2)])
        over_y = low + columns_on(high)
        forces.append(columns_on(over_x) - over_x + rows_down(over_y) - over_y)
    return forces


def law(strain, harden):
    volume = strain[0] + strain[1]
    normal = 0.5 * (strain[0] - strain[1])
    shear = 0.5 * strain[2]
    stiff = harden * (2.0 * normal * normal + 2.0 * shear * shear)
    factor = (1.0 + 2.0 * stiff) / (1.0 + 3.0 * stiff)
    for turn in range(2):
        square = stiff * factor * factor
        factor = (1.0 + 2.0 * square * factor) / (1.0 + 3.0 * square)
    square = factor * factor
    slope = -harden * square * factor / (1.0 + 3.0 * stiff * square)
    return volume, normal, shear, factor, slope


def stress_of(state, bulk, modulus):
    volume, normal, shear, factor, slope = state
    spread = 2.0 * modulus * factor
    return [bulk * volume + spread * normal, bulk * volume - spread * normal, spread * shear]


def image_of(state, bulk, modulus, rest):
    volume, normal, shear, factor, slope = state
    d_volume = rest[0] + rest[1]
    d_normal = 0.5 * (rest[0] - rest[1])
    d_shear = 0.5 * rest[2]
    d_factor = slope * (4.0 * normal * d_normal + 4.0 * shear * d_shear)
    d_dev = 2.0 * modulus * (factor * d_normal + d_factor * normal)
    return [
        bulk * d_volume + d_dev,
        bulk * d_volume - d_dev,
        2.0 * modulus * (factor * d_shear + d_factor * shear),
    ]


def green(first, second, mixed, part_11, part_22, cross):
    across = cross * mixed
    total = part_11 * first + 2.0 * across + part_22 * second
    out_11 = (part_11 * first + across) * (1.0 / MU_REF) - COUPLE * part_11 * total
    out_22 = (across + part_22 * second) * (1.0 / MU_REF) - COUPLE * part_22 * total
    out_12 = (cross * (first + second) + (part_11 + part_22) * mixed) * (
        1.0 / MU_REF
    ) - 2.0 * COUPLE * cross * total
    return out_11, out_22, out_12


def kernel(
    disp, body, assign, phase, flag, table_hbm,
    correction_out, strain_out, hom_out,
    table, pf, a1src, a1, nb, a2src, a2, c1src, c1, c2src, c2, d1src, d1, d2src, d2,
    halo_u, halo_f, halo_a,
    parts, labels, accs, green_tab, ph_f, hard_f, ind_h, mid_h, mid_l, spec, filt_h, filt_l,
    strains, last, basis, tangent,
    sem_table, send, recv, gather_recv, halo_recv,
):
    r = lax.axis_index("rve")
    s = lax.axis_index("slab")
    y, core = s // 2, s % 2
    half, lane_field = s // 4, s % 4
    before, after = lax.rem(r + GROUPS - 1, GROUPS), lax.rem(r + 1, GROUPS)
    left = (jnp.where(s == 0, before, r), lax.rem(s + SLABS - 1, SLABS))
    right = (jnp.where(s == SLABS - 1, after, r), lax.rem(s + 1, SLABS))

    table_copy = pltpu.make_async_copy(table_hbm, table, sem_table)
    table_copy.start()

    barrier = pltpu.get_barrier_semaphore()

    def greet(device):
        pl.semaphore_signal(barrier, inc=1, device_id=device, device_id_type=MESH)

    for k in range(1, SLABS):
        greet((r, lax.rem(s + k, SLABS)))
    greet((after, 0))

    @pl.when(s == 0)
    def _():
        for k in range(SLABS):
            greet((before, k))

    for k in range(1, GROUPS):
        greet((lax.rem(r + k, GROUPS), s))

    pf[core, y, 0] = phase[...]
    pf[core, y, 1] = flag[...]

    def label_sums(rows, count):
        step = rows // 8

        def one(label, _):
            e = [parts[k, 0:rows, :] for k in range(8)]
            mask = [jnp.where(labels[p, 0:rows, :] == label.astype(F32), 1.0, 0.0) for p in range(4)]
            t_low, t_high = mask[0] + mask[1], mask[2] + mask[3]
            s_low, s_high = mask[0] + mask[2], mask[1] + mask[3]
            sums = [
                e[0] * t_low + e[1] * t_high,
                e[2] * s_low + e[3] * s_high,
                e[4] * s_low + e[5] * s_high + e[6] * t_low + e[7] * t_high,
            ]
            if count:
                sums.append(t_low + t_high)
            for c in range(len(sums)):
                accs[c, label] = jnp.sum(sums[c].reshape(step, 8, 128), axis=0)
            return 0

        lax.fori_loop(0, GROUPS, one, 0, unroll=4)
        if not count:
            accs[3] = jnp.zeros((GROUPS, 8, 128), F32)
        folded = jnp.sum(accs[...].reshape(4 * GROUPS, 8, 128), axis=1)
        ones = jnp.ones((8, 128), F32)
        return lax.dot_general(
            ones, folded, (((1,), (1,)), ((), ())),
            precision=lax.Precision.HIGHEST, preferred_element_type=F32,
        )[0:1, :]

    def keep_parts(fields, rows):
        d1x, d2y, d1y, d2x = strain_parts(*fields)
        for k, value in enumerate(d1x + d2y + d1y + d2x):
            parts[k, 0:rows, :] = value

    row_of = lax.broadcasted_iota(jnp.int32, (BLOCK, 128), 0)
    own = [disp[0], disp[1]]
    beside = [jnp.where(row_of == BLOCK - 1, 0.0, columns_back(u)) for u in own]
    keep_parts(own + beside, BLOCK)
    for p in range(4):
        labels[p] = assign[p].astype(F32)
    a1src[...] = jnp.concatenate(
        [label_sums(BLOCK, True), disp[0, 0:1, :], disp[1, 0:1, :]]
        + [labels[p, BLOCK - 1 : BLOCK, :] for p in range(4)]
        + [jnp.zeros((1, 128), F32)],
        axis=0,
    )
    a1[s] = a1src[...]

    def symbols(k, _):
        rows = pl.ds(pl.multiple_of(k * 32, 32), 32)
        row = lax.broadcasted_iota(jnp.int32, (32, GRID), 0) + k * 32
        lane = lax.broadcasted_iota(jnp.int32, (32, GRID), 1)
        k1 = lax.rem(row, HALF).astype(F32)
        k2 = lax.rem(lane, HALF).astype(F32)
        square = k1 * k1 + k2 * k2
        inverse = jnp.where(square > 0.0, 1.0 / jnp.maximum(square, 1.0), 0.0)
        sign = jnp.where((row < HALF) == (lane < HALF), -1.0, 1.0)
        green_tab[0, rows, :] = k1 * k1 * inverse
        green_tab[1, rows, :] = k2 * k2 * inverse
        green_tab[2, rows, :] = sign * k1 * k2 * inverse
        return 0

    lax.fori_loop(0, 8, symbols, 0)

    pl.semaphore_wait(barrier, SLABS - 1 + GROUPS - 1 + 1 + jnp.where(s == 0, SLABS, 0))

    def push(source, target, k, recv_sem, device):
        pltpu.make_async_remote_copy(
            source, target, send.at[k], recv_sem, device_id=device, device_id_type=MESH
        ).start()

    def drained(ref, sem):
        pltpu.make_async_copy(ref, ref, sem).wait()

    for k in range(1, SLABS):
        push(a1src, a1.at[s], 0, recv.at[0], (r, lax.rem(s + k, SLABS)))

    @pl.when(s == 0)
    def _():
        for k in range(SLABS):
            push(a1src, nb, 1, recv.at[1], (before, k))

    sibling = (r, y * 2 + 1 - core)
    for k in range(1, 4):
        push(pf.at[core, y], pf.at[core, y], 2, gather_recv.at[y], (r, lax.rem(y + k, 4) * 2 + core))
    push(pf.at[core, y], pf.at[core, y], 3, recv.at[2], sibling)

    for k, (own_ref, halo) in enumerate(((disp, halo_u), (body, halo_f), (assign, halo_a))):
        push(own_ref.at[:, pl.ds(0, 8), :], halo.at[1], 4 + 2 * k, halo_recv.at[k, 1], left)
        push(own_ref.at[:, pl.ds(BLOCK - 8, 8), :], halo.at[0], 5 + 2 * k, halo_recv.at[k, 0], right)

    drained(a1.at[pl.ds(0, SLABS - 1)], recv.at[0])
    drained(nb, recv.at[1])
    row8 = lax.broadcasted_iota(jnp.int32, (8, 128), 0)
    gathered = a1[...]
    at_end = jnp.where(r == GROUPS - 1, 0.0, 1.0)
    nxt = []
    for c in range(2):
        own_c = jnp.concatenate([gathered[k, 1 + c : 2 + c, :] for k in range(SLABS)], axis=0)
        nxt.append(jnp.where(row8 == 7, nb[1 + c : 2 + c, :] * at_end, columns_back(own_c)))
    zero8 = jnp.zeros((8, 128), F32)
    keep_parts([zero8, zero8] + nxt, 8)
    for p in range(4):
        labels[p, 0:8, :] = jnp.concatenate([gathered[k, 3 + p : 4 + p, :] for k in range(SLABS)], axis=0)
    a2src[...] = label_sums(8, False) + jnp.sum(gathered, axis=0)[0:1, :]
    a2[r] = a2src[...]
    for k in range(1, GROUPS):
        push(a2src, a2.at[r], 10, recv.at[3], (lax.rem(r + k, GROUPS), s))

    for k in range(1, 4):
        other = lax.rem(y + k, 4)
        drained(pf.at[core, other], gather_recv.at[other])
        push(pf.at[core, other], pf.at[core, other], 3, recv.at[2], sibling)
    drained(pf.at[1 - core], recv.at[2])

    for yy in range(4):
        for cc in range(2):
            rows = slice((yy * 2 + cc) * BLOCK, (yy * 2 + cc + 1) * BLOCK)
            here = pf[cc, yy, 0].astype(F32)
            active = pf[cc, yy, 1].astype(F32)
            ph_f[rows, :] = here
            hard_f[rows, :] = active * (2.0 - 1.5 * here)
            ind_h[0, rows, :] = here.astype(BF16)
            ind_h[1, rows, :] = active.astype(BF16)
            ind_h[2, rows, :] = (here * active).astype(BF16)

    table_copy.wait()

    def along_x(high, low, rows=slice(None), which=0):
        left_h, left_l = table[which, rows, :], table[which + 1, rows, :]
        return dot(left_h, high) + dot(left_h, low) + dot(left_l, high)

    def along_y(high, low, which):
        right_h, right_l = table[which], table[which + 1]
        return dot(high, right_h) + dot(high, right_l) + dot(low, right_h)

    for m in range(3):
        value = dot(ind_h[m], table[2]) + dot(ind_h[m], table[3])
        mid_h[m], mid_l[m] = split(value)
    for m in range(3):
        spec[m] = along_x(mid_h[m], mid_l[m])

    drained(a2.at[pl.ds(0, GROUPS - 1)], recv.at[3])
    totals = jnp.sum(a2[...], axis=0)
    lane1 = lane_iota((1, 128))
    picked = [
        jnp.sum(jnp.where(lane1 == 32 * c + r, totals, 0.0), axis=1, keepdims=True) for c in range(4)
    ]
    mean = [jnp.broadcast_to(picked[c] / picked[3], (8, 128)) for c in range(3)]
    unit = [jnp.where(lane_field == c, 1.0, 0.0) + jnp.where((lane_field == 3) & (c == 2), 1.0, 0.0) for c in range(3)]
    units = [jnp.full((8, 128), u, F32) for u in unit]

    kinds = {}
    for p in range(2):
        bulk, modulus = (6.0, 3.0) if p else (2.0, 1.0)
        for f in range(2):
            state = law(mean, (0.5 if p else 2.0) * f)
            kinds[p, f] = stress_of(state, bulk, modulus) + image_of(state, bulk, modulus, units)
    weights = []
    for k in range(6):
        base = kinds[0, 0][k]
        by_phase = kinds[1, 0][k] - base
        by_flag = kinds[0, 1][k] - base
        weights.append((by_phase, by_flag, kinds[1, 1][k] - base - by_phase - by_flag))

    def filter_all(load):
        def rows_of(k, _):
            for a in range(2):
                rows = pl.ds(pl.multiple_of(a * HALF + k * 16, 16), 16)
                swap_rows = pl.ds(pl.multiple_of((1 - a) * HALF + k * 16, 16), 16)
                for b in range(2):
                    lanes = slice(b * HALF, (b + 1) * HALF)
                    swap_lanes = slice((1 - b) * HALF, (2 - b) * HALF)
                    sym = [green_tab[i, rows, lanes] for i in range(3)]
                    firsts, seconds, mixeds = load(rows, lanes, swap_rows, swap_lanes)
                    for n in range(2):
                        out = green(firsts[n], seconds[n], mixeds[n], *sym)
                        for c in range(3):
                            rr, ll = (swap_rows, swap_lanes) if c == 2 else (rows, lanes)
                            high, low = split(out[c])
                            filt_h[3 * n + c, rr, ll] = high
                            filt_l[3 * n + c, rr, ll] = low
            return 0

        lax.fori_loop(0, 8, rows_of, 0)

    def wide(value):
        return jnp.concatenate([value, value], axis=0)

    wide_weights = [[wide(w) for w in three] for three in weights]

    def load_first(rows, lanes, swap_rows, swap_lanes):
        here = [spec[m, rows, lanes] for m in range(3)]
        there = [spec[m, swap_rows, swap_lanes] for m in range(3)]
        mix = lambda k, fields: sum(wide_weights[k][m] * fields[m] for m in range(3))
        return (
            [mix(0, here), mix(3, here)],
            [mix(1, here), mix(4, here)],
            [mix(2, there), mix(5, there)],
        )

    filter_all(load_first)

    start = mean + units
    for k in range(6):
        high, low = split(along_x(filt_h[k], filt_l[k], which=2))
        strains[k] = jnp.broadcast_to(start[k][0:1, 0:1], (GRID, GRID)) - along_y(high, low, 0)

    def material(k, _):
        rows = pl.ds(pl.multiple_of(k * 16, 16), 16)
        for b in range(2):
            lanes = slice(b * HALF, (b + 1) * HALF)
            here = ph_f[rows, lanes]
            state = law([strains[c, rows, lanes] for c in range(3)], hard_f[rows, lanes])
            bulk, modulus = 2.0 + 4.0 * here, 1.0 + 2.0 * here
            values = stress_of(state, bulk, modulus) + image_of(
                state, bulk, modulus, [strains[3 + c, rows, lanes] for c in range(3)]
            )
            for c in range(6):
                filt_h[c, rows, lanes], filt_l[c, rows, lanes] = split(values[c])
        return 0

    lax.fori_loop(0, 16, material, 0)
    for k in range(6):
        mid_h[k], mid_l[k] = split(along_y(filt_h[k], filt_l[k], 2))
    for k in range(6):
        spec[k] = along_x(mid_h[k], mid_l[k])

    def load_second(rows, lanes, swap_rows, swap_lanes):
        return (
            [spec[0, rows, lanes], spec[3, rows, lanes]],
            [spec[1, rows, lanes], spec[4, rows, lanes]],
            [spec[2, swap_rows, swap_lanes], spec[5, swap_rows, swap_lanes]],
        )

    filter_all(load_second)
    part = pl.ds(pl.multiple_of(half * HALF, HALF), HALF)
    for k in range(6):
        high, low = split(along_x(filt_h[k], filt_l[k], rows=part, which=2))
        last[k] = strains[k, part, :] - along_y(high, low, 0)

    def finish(k, sums):
        rows = pl.ds(pl.multiple_of(k * 16, 16), 16)
        full = pl.ds(pl.multiple_of(half * HALF + k * 16, 16), 16)
        sums = list(sums)
        for b in range(2):
            lanes = slice(b * HALF, (b + 1) * HALF)
            here = ph_f[full, lanes]
            state = law([last[c, rows, lanes] for c in range(3)], hard_f[full, lanes])
            bulk, modulus = 2.0 + 4.0 * here, 1.0 + 2.0 * here
            values = stress_of(state, bulk, modulus) + image_of(
                state, bulk, modulus, [last[3 + c, rows, lanes] for c in range(3)]
            )
            for c in range(6):
                sums[c] = sums[c] + values[c][0:8, :] + values[c][8:16, :]
        return tuple(sums)

    sums = lax.fori_loop(0, 8, finish, tuple(jnp.zeros((8, 128), F32) for c in range(6)))
    strain_out[0] = last[0:3, pl.ds(pl.multiple_of(lane_field * BLOCK, BLOCK), BLOCK), :]

    message = jnp.zeros((1, 128), F32)
    for c in range(3):
        stress_sum, image_sum = [
            jnp.sum(jnp.sum(sums[k], axis=0, keepdims=True), axis=1, keepdims=True) * (1.0 / (GRID * GRID))
            for k in (c, 3 + c)
        ]
        message = message + jnp.where((lane1 == c) & (lane_field == 0), stress_sum, 0.0)
        message = message + jnp.where((lane1 == 3 + 3 * lane_field + c) & (lane_field < 3), image_sum, 0.0)
        message = message + jnp.where((lane1 == 12 + c) & (s == 0), mean[c][0:1, :], 0.0)
    c1src[...] = message
    c1[s] = message
    for k in range(1, SLABS):
        push(c1src, c1.at[s], 11, recv.at[4], (r, lax.rem(s + k, SLABS)))

    for k, halo in enumerate((halo_u, halo_f, halo_a)):
        drained(halo.at[0], halo_recv.at[k, 0])
        drained(halo.at[1], halo_recv.at[k, 1])
    column = lax.broadcasted_iota(jnp.int32, (EXT, 128), 0) + ((r * SLABS + s) * BLOCK - 8)
    inside = (column >= 0) & (column < GROUPS * SLABS * BLOCK)

    def extended(halo, own_ref, c):
        return jnp.concatenate([halo[0, c], own_ref[c], halo[1, c]], axis=0)

    u = [jnp.where(inside, extended(halo_u, disp, c), 0.0) for c in range(2)]
    force = [extended(halo_f, body, c) for c in range(2)]
    index = [jnp.where(inside, extended(halo_a, assign, p), 127) for p in range(4)]
    u_parts = strain_parts(u[0], u[1], columns_back(u[0]), columns_back(u[1]))

    drained(c1.at[pl.ds(0, SLABS - 1)], recv.at[4])
    c2src[...] = jnp.sum(c1[...], axis=0)
    c2[r] = c2src[...]
    for k in range(1, GROUPS):
        push(c2src, c2.at[r], 12, recv.at[5], (lax.rem(r + k, GROUPS), s))
    drained(c2.at[pl.ds(0, GROUPS - 1)], recv.at[5])
    square = jnp.concatenate([c2[...].reshape(GROUPS, 128), jnp.zeros((128 - GROUPS, 128), F32)], axis=0)
    by_label = square.T[0:16, :]
    hom_out[...] = by_label[0:12, 0:GROUPS]
    rows = [by_label[k : k + 1, :] for k in range(15)]
    offset = [rows[c] - sum(rows[3 + 3 * j + c] * rows[12 + j] for j in range(3)) for c in range(3)]
    size = sum(jnp.abs(rows[k]) for k in range(3, 12))
    scale = RANGE * jnp.max(size, axis=1, keepdims=True)
    inverse_scale = 1.0 / scale

    def looked(row, p):
        return jnp.take_along_axis(jnp.broadcast_to(row, (EXT, 128)), index[p], axis=1, mode="promise_in_bounds")

    def point_strain(shapes, p):
        d1x, d2y, d1y, d2x = shapes
        sp, tp = p % 2, p // 2
        return d1x[tp], d2y[sp], d1y[sp] + d2x[tp]

    stress = []
    for p in range(4):
        strain = point_strain(u_parts, p)
        cs = [looked(rows[3 + k], p) for k in range(9)]
        for k in range(9):
            tangent[p, k] = cs[k]
        stress.append(
            [
                looked(offset[c], p) + cs[c] * strain[0] + cs[3 + c] * strain[1] + cs[6 + c] * strain[2]
                for c in range(3)
            ]
        )
    forces = assemble(stress)
    vector = [jnp.where(inside, force[c] - forces[c], 0.0) for c in range(2)]
    history = [vector]
    basis[0, 0], basis[0, 1] = vector[0][8:40], vector[1][8:40]

    def stiffness(field):
        shapes = strain_parts(field[0], field[1], columns_back(field[0]), columns_back(field[1]))
        result = []
        for p in range(4):
            strain = point_strain(shapes, p)
            result.append(
                [
                    tangent[p, c] * strain[0] + tangent[p, 3 + c] * strain[1] + tangent[p, 6 + c] * strain[2]
                    for c in range(3)
                ]
            )
        return assemble(result)

    for k in range(CG_STEPS):
        image = stiffness(history[k])
        shifted = [jnp.where(inside, image[c] * inverse_scale - history[k][c], 0.0) for c in range(2)]
        if k:
            shifted = [2.0 * shifted[c] - history[k - 1][c] for c in range(2)]
        history.append(shifted)
        basis[k + 1, 0], basis[k + 1, 1] = shifted[0][8:40], shifted[1][8:40]

    dots = []
    for i, j in PAIRS:
        product = basis[i, 0] * basis[j, 0] + basis[i, 1] * basis[j, 1]
        dots.append(jnp.sum(product.reshape(4, 8, 128), axis=(0, 1), keepdims=True).reshape(1, 128))
    dots += [jnp.zeros((1, 128), F32)] * (16 - len(dots))
    stacked = jnp.sum(jnp.concatenate(dots, axis=0), axis=1, keepdims=True)
    diagonal = lax.broadcasted_iota(jnp.int32, (16, 128), 0) == lane_iota((16, 128))
    d1src[...] = jnp.sum(jnp.where(diagonal, stacked, 0.0), axis=0, keepdims=True)
    d1[s] = d1src[...]
    for k in range(1, SLABS):
        push(d1src, d1.at[s], 13, recv.at[6], (r, lax.rem(s + k, SLABS)))
    drained(d1.at[pl.ds(0, SLABS - 1)], recv.at[6])
    d2src[...] = jnp.sum(d1[...], axis=0)
    d2[r] = d2src[...]
    for k in range(1, GROUPS):
        push(d2src, d2.at[r], 14, recv.at[7], (lax.rem(r + k, GROUPS), s))
    drained(d2.at[pl.ds(0, GROUPS - 1)], recv.at[7])
    gram_row = jnp.sum(d2[...], axis=0)
    gram = {}
    for k, (i, j) in enumerate(PAIRS):
        value = jnp.sum(jnp.where(lane1 == k, gram_row, 0.0), axis=1, keepdims=True)
        gram[i, j] = gram[j, i] = value

    def inner(one, two):
        return sum(one[i] * two[j] * gram[i, j] for i in range(len(one)) for j in range(len(two)))

    def apply(coefficients):
        n = len(coefficients)
        result = [scale * c for c in coefficients] + [0.0]
        for k in range(n):
            if k == 0:
                result[1] = result[1] + scale * coefficients[0]
            else:
                result[k + 1] = result[k + 1] + 0.5 * scale * coefficients[k]
                result[k - 1] = result[k - 1] + 0.5 * scale * coefficients[k]
        return result

    one = jnp.ones((1, 1), F32)
    direction, residual = [one], [one]
    answer = []
    rho = gram[0, 0]
    for step in range(CG_STEPS):
        image = apply(direction)
        alpha = rho / inner(direction, image)
        answer = [
            (answer[k] if k < len(answer) else 0.0) + alpha * direction[k] for k in range(len(direction))
        ]
        if step == CG_STEPS - 1:
            break
        residual = [
            (residual[k] if k < len(residual) else 0.0) - alpha * image[k] for k in range(len(image))
        ]
        fresh = inner(residual, residual)
        beta = fresh / rho
        direction = [
            residual[k] + (beta * direction[k] if k < len(direction) else 0.0) for k in range(len(residual))
        ]
        rho = fresh
    for c in range(2):
        correction_out[c] = sum(answer[k] * basis[k, c] for k in range(CG_STEPS))

    drained(a1.at[pl.ds(0, SLABS - 1)], send.at[0])

    @pl.when(s == 0)
    def _():
        drained(a1, send.at[1])

    drained(pf.at[0, pl.ds(0, 3)], send.at[2])
    drained(pf.at[0], send.at[3])
    for k, halo in enumerate((halo_u, halo_f, halo_a)):
        drained(halo.at[1], send.at[4 + 2 * k])
        drained(halo.at[0], send.at[5 + 2 * k])
    drained(a2.at[pl.ds(0, GROUPS - 1)], send.at[10])
    drained(c1.at[pl.ds(0, SLABS - 1)], send.at[11])
    drained(c2.at[pl.ds(0, GROUPS - 1)], send.at[12])
    drained(d1.at[pl.ds(0, SLABS - 1)], send.at[13])
    drained(d2.at[pl.ds(0, GROUPS - 1)], send.at[14])


def shards(displacement, body_force, assignment, phases, flags):
    tables = jnp.asarray(transform_tables())
    vmem = pl.BlockSpec(memory_space=pltpu.VMEM)
    row = lambda n: pltpu.VMEM((n, 1, 128), F32)
    one_row = pltpu.VMEM((1, 128), F32)
    square = (GRID, GRID)
    correction, strain, hom = pl.pallas_call(
        kernel,
        out_shape=(
            jax.ShapeDtypeStruct((2, BLOCK, 128), F32),
            jax.ShapeDtypeStruct((1, 3, BLOCK, GRID), F32),
            jax.ShapeDtypeStruct((12, GROUPS), F32),
        ),
        in_specs=[vmem] * 5 + [pl.BlockSpec(memory_space=pl.ANY)],
        out_specs=(vmem, vmem, vmem),
        scratch_shapes=[
            pltpu.VMEM((4,) + square, BF16),
            pltpu.VMEM((2, 4, 2, BLOCK, GRID), jnp.int32),
            pltpu.VMEM((8, 128), F32),
            pltpu.VMEM((SLABS, 8, 128), F32),
            pltpu.VMEM((8, 128), F32),
            one_row, row(GROUPS), one_row, row(SLABS), one_row, row(GROUPS),
            one_row, row(SLABS), one_row, row(GROUPS),
            pltpu.VMEM((2, 2, 8, 128), F32),
            pltpu.VMEM((2, 2, 8, 128), F32),
            pltpu.VMEM((2, 4, 8, 128), jnp.int32),
            pltpu.VMEM((8, BLOCK, 128), F32),
            pltpu.VMEM((4, BLOCK, 128), F32),
            pltpu.VMEM((4, GROUPS, 8, 128), F32),
            pltpu.VMEM((3,) + square, F32),
            pltpu.VMEM(square, F32),
            pltpu.VMEM(square, F32),
            pltpu.VMEM((3,) + square, BF16),
            pltpu.VMEM((6,) + square, BF16),
            pltpu.VMEM((6,) + square, BF16),
            pltpu.VMEM((6,) + square, F32),
            pltpu.VMEM((6,) + square, BF16),
            pltpu.VMEM((6,) + square, BF16),
            pltpu.VMEM((6,) + square, F32),
            pltpu.VMEM((6, HALF, GRID), F32),
            pltpu.VMEM((CG_STEPS + 1, 2, BLOCK, 128), F32),
            pltpu.VMEM((4, 9, EXT, 128), F32),
            pltpu.SemaphoreType.DMA,
            pltpu.SemaphoreType.DMA((15,)),
            pltpu.SemaphoreType.DMA((8,)),
            pltpu.SemaphoreType.DMA((4,)),
            pltpu.SemaphoreType.DMA((3, 2)),
        ],
        compiler_params=pltpu.CompilerParams(
            collective_id=0, has_side_effects=True, vmem_limit_bytes=48 * 1024 * 1024
        ),
        name="fe2_step",
    )(displacement, body_force, assignment, phases[0], flags[0], tables)
    return correction, strain, hom


def solution(mesh):
    return jax.shard_map(
        shards,
        mesh=mesh,
        in_specs=(
            P(None, ("rve", "slab"), None),
            P(None, ("rve", "slab"), None),
            P(None, ("rve", "slab"), None),
            P("rve", "slab", None),
            P("rve", "slab", None),
        ),
        out_specs=(P(None, ("rve", "slab"), None), P("rve", None, "slab", None), P()),
        check_vma=False,
    )
```

time: 1040 us -> 57.3 us (0.06)
  blocking collectives: 678 us -> 0 us
  local copies, waits for them, and re-layouts: 167 us -> 6.76 us
  Pallas kernels: 0 us -> 49.5 us
  starting transfers between devices: 46.7 us -> 0 us
  waiting for transfers between devices: 45.4 us -> 0 us
  other arithmetic: 38 us -> 0 us
  matrix products: 37.4 us -> 0 us
  between operations: 16.2 us -> 0.65 us
    psum x9 -> x0, blocking collectives: 634 us -> none  [the longest x7 540 us: inner_product(): return lax.psum(jnp.sum(left * right), ('rve', 'slab'))]
    gather x16 -> x0, local copies, waits for them, and re-layouts: 101 us -> none  [the longest x8 55.4 us: stiffness(): tangent = jnp.take(homogenised[3:12], assignment[index], axis=1)]
    pallas_call x0 -> x1, Pallas kernels: none -> 49.5 us  [shards(): pl.pallas_call(kernel, out_shape=(jax.ShapeDtypeStruct((2, BLOCK, 128), F...]
    dot_general x28 -> x0, matrix products: 37.4 us -> none  [the longest x2 3.67 us: shards(): jnp.einsum('kx,ncxy->ncky', sin_table, filt_real, precision=HIGHEST)]
    all_to_all x3 -> x0, waiting for transfers between devices: 33.6 us -> none  [the longest x2 21.6 us: shards(): lax.all_to_all(jnp.stack([back_real, back_imag], 1), 'slab', split_axis=3...]
    ppermute x10 -> x0, starting transfers between devices: 33.5 us -> none  [passed_along(): lax.ppermute(value, axis, [(source, source + steps) for source in range(l...]
    all_gather x1 -> x0, blocking collectives: 27.9 us -> none  [shards(): totals = lax.all_gather(group[:, None], 'rve', axis=1, tiled=True)]
    all_to_all x9 -> x0, local copies, waits for them, and re-layouts: 24.7 us -> none  [the longest x5 12.6 us: shards(): lax.all_to_all(spectrum, 'slab', split_axis=4, concat_axis=3, tiled=True)]
  transfers between devices with their start and end apart: 13 -> 0, of which waited for: 11 -> 0; matrix products, arithmetic and copies ran while one was open for 2% -> 0% of each run, Pallas kernels for 0% -> 0%
where the time goes in v1:
time: 57.3 us; the launch traced here: 56.9 us
  Pallas kernels  49.5 us (86%)
  local copies, waits for them, and re-layouts  6.76 us (12%)
  between operations  0.65 us (1%)
    pallas_call x1, Pallas kernels, shards(): pl.pallas_call(kernel, out_shape=(jax.ShapeDtypeStruct((2, BLOCK, 128), F...  49.5 us
    unnamed x15, local copies, waits for them, and re-layouts  6.76 us

profile of v1, /device:TPU:1, one launch (start us, length us, event | category | flops | bytes accessed | tf_op | source)
XLA Modules:
  0.0 56.9 jit_solution(1319414396085296700)
XLA Ops:
  0.6 0.0 copy-start
  0.6 1.0 %copy-done = bf16[4,256,256]{2,1,0:T(8,128)(2,1)S(1)} copy-done((bf16[4,256,256]{2,1,0:T(8,128)(2,1)S(1)}, bf16[4,256,256]{2,1,0:T(8,128)(2,1)}, u32[]{:S(2)}) %copy-start) | copy-done | bytes 524312
  1.7 0.0 copy-start.1
  1.7 0.8 %copy-done.1 = s32[4,32,128]{2,1,0:T(8,128)S(1)} copy-done((s32[4,32,128]{2,1,0:T(8,128)S(1)}, s32[4,32,128]{2,1,0:T(8,128)}, u32[]{:S(2)}) %copy-start.1) | copy-done | bytes 65560
  2.5 0.0 copy-start.2
  2.5 0.8 %copy-done.2 = f32[2,32,128]{2,1,0:T(8,128)S(1)} copy-done((f32[2,32,128]{2,1,0:T(8,128)S(1)}, f32[2,32,128]{2,1,0:T(8,128)}, u32[]{:S(2)}) %copy-start.2) | copy-done | bytes 32792
  3.3 0.0 copy-start.3
  3.3 0.8 %copy-done.3 = f32[2,32,128]{2,1,0:T(8,128)S(1)} copy-done((f32[2,32,128]{2,1,0:T(8,128)S(1)}, f32[2,32,128]{2,1,0:T(8,128)}, u32[]{:S(2)}) %copy-start.3) | copy-done | bytes 32792
  4.0 0.0 copy-start.4
  4.0 0.8 %copy-done.4 = s32[1,32,256]{2,1,0:T(8,128)S(1)} copy-done((s32[1,32,256]{2,1,0:T(8,128)S(1)}, s32[1,32,256]{2,1,0:T(8,128)}, u32[]{:S(2)}) %copy-start.4) | copy-done | bytes 32792
  4.8 0.0 copy-start.5
  4.8 0.8 %copy-done.5 = s32[1,32,256]{2,1,0:T(8,128)S(1)} copy-done((s32[1,32,256]{2,1,0:T(8,128)S(1)}, s32[1,32,256]{2,1,0:T(8,128)}, u32[]{:S(2)}) %copy-start.5) | copy-done | bytes 32792
  5.6 49.5 %fe2_step.1 = (f32[2,32,128]{2,1,0:T(8,128)S(1)}, f32[1,3,32,256]{3,2,1,0:T(8,128)S(1)}, f32[12,32]{1,0:T(8,128)S(1)}) custom-call(f32[2,32,128]{2,1,0:T(8,128)S(1)} %copy-done.2, f32[2,32,128]{2,1,0:T(8,128)S(1)} %copy-done.3, s32[4,32,128]{2,1,0:T(8,128)S(1)} %copy-done.1, s32[32,256]{1,0:T(8,128)S(1)} %bitcast.2, s32[32,256]{1,0:T(8,128)S(1)} %bitcast.3, ...), custom_call_target="tpu_custom_call" | custom-call | tf_op jit(solution)/shard_map/fe2_step/pallas_call | solution.py:640
  55.0 0.6 %copy.12 = f32[2,32,128]{2,1,0:T(8,128)} copy(f32[2,32,128]{2,1,0:T(8,128)S(1)} %get-tuple-element.6) | data formatting | bytes 65536
  55.7 0.6 %copy.13 = f32[1,3,32,256]{3,2,1,0:T(8,128)} copy(f32[1,3,32,256]{3,2,1,0:T(8,128)S(1)} %get-tuple-element.7) | data formatting | bytes 196608
  56.3 0.6 %copy.14 = f32[12,32]{1,0:T(8,128)} copy(f32[12,32]{1,0:T(8,128)S(1)} %get-tuple-element.8) | data formatting | bytes 3072
Async XLA Ops:
  0.6 1.0 %copy-start = (bf16[4,256,256]{2,1,0:T(8,128)(2,1)S(1)}, bf16[4,256,256]{2,1,0:T(8,128)(2,1)}, u32[]{:S(2)}) copy-start(bf16[4,256,256]{2,1,0:T(8,128)(2,1)} %constant.2.clone.table_hbm) | copy-start | bytes 1572868
  1.7 0.8 %copy-start.1 = (s32[4,32,128]{2,1,0:T(8,128)S(1)}, s32[4,32,128]{2,1,0:T(8,128)}, u32[]{:S(2)}) copy-start(s32[4,32,128]{2,1,0:T(8,128)} %assign.1) | copy-start | bytes 196612
  2.5 0.8 %copy-start.2 = (f32[2,32,128]{2,1,0:T(8,128)S(1)}, f32[2,32,128]{2,1,0:T(8,128)}, u32[]{:S(2)}) copy-start(f32[2,32,128]{2,1,0:T(8,128)} %disp.1) | copy-start | bytes 98308
  3.3 0.8 %copy-start.3 = (f32[2,32,128]{2,1,0:T(8,128)S(1)}, f32[2,32,128]{2,1,0:T(8,128)}, u32[]{:S(2)}) copy-start(f32[2,32,128]{2,1,0:T(8,128)} %body.1) | copy-start | bytes 98308
  4.0 0.8 %copy-start.4 = (s32[1,32,256]{2,1,0:T(8,128)S(1)}, s32[1,32,256]{2,1,0:T(8,128)}, u32[]{:S(2)}) copy-start(s32[1,32,256]{2,1,0:T(8,128)} %param.9) | copy-start | bytes 98308
  4.8 0.8 %copy-start.5 = (s32[1,32,256]{2,1,0:T(8,128)S(1)}, s32[1,32,256]{2,1,0:T(8,128)}, u32[]{:S(2)}) copy-start(s32[1,32,256]{2,1,0:T(8,128)} %param.10) | copy-start | bytes 98308

commit v2 on v1

--- a/solution.py
+++ b/solution.py
@@ -2,8 +2,6 @@
 
 import jax
 import jax.numpy as jnp
-import ml_dtypes
-import numpy as np
 from jax import lax
 from jax.experimental import pallas as pl
 from jax.experimental.pallas import tpu as pltpu
@@ -33,25 +31,27 @@
 PAIRS = [(i, j) for i in range(CG_STEPS) for j in range(i, CG_STEPS + 1)]
 
 
-def transform_tables():
-    n = GRID
-    place = np.arange(n)
-    rows = []
-    for slot in range(n):
-        if slot < HALF:
-            scale = math.sqrt((1.0 if slot == 0 else 2.0) / n)
-            rows.append(scale * np.cos(2.0 * np.pi * (slot * place % n) / n))
-        elif slot == HALF:
-            rows.append(math.sqrt(1.0 / n) * np.cos(np.pi * place))
-        else:
-            rows.append(math.sqrt(2.0 / n) * np.sin(2.0 * np.pi * ((slot - HALF) * place % n) / n))
-    forward = np.stack(rows).astype(np.float32)
-    tables = []
-    for table in (forward, forward.T):
-        high = table.astype(ml_dtypes.bfloat16)
-        low = (table - high.astype(np.float32)).astype(ml_dtypes.bfloat16)
-        tables += [high, low]
-    return np.stack(tables)
+def wave(slot, place):
+    k = jnp.where(slot == HALF, HALF, lax.rem(slot, HALF))
+    sine = slot > HALF
+    turn = lax.bitwise_and(k * place + jnp.where(sine, 3 * GRID // 4, 0), GRID - 1)
+    angle = (jnp.abs(turn - HALF) - GRID // 4).astype(F32) * (2.0 * math.pi / GRID)
+    square = angle * angle
+    value = 1.0 / 362880.0 - square * (1.0 / 39916800.0)
+    for term in (1.0 / 5040.0, 1.0 / 120.0, 1.0 / 6.0, 1.0):
+        value = term - square * value
+    flat = (k == 0) | (k == HALF)
+    return angle * value * jnp.where(flat, 1.0 / math.sqrt(GRID), math.sqrt(2.0 / GRID))
+
+
+OFFSETS = sorted(
+    ((dx, dz) for dx in range(4) for dz in range(8) if dx or dz),
+    key=lambda o: -(min(o[0], 4 - o[0]) + min(o[1], 8 - o[1])),
+)
+NEAR = sorted(
+    ((dy, dc) for dy in range(4) for dc in range(2) if dy or dc),
+    key=lambda o: (-min(o[0], 4 - o[0]), -o[1]),
+)
 
 
 def lane_iota(shape):
@@ -118,17 +118,22 @@
     return forces
 
 
+def inverse(value):
+    guess = pl.reciprocal(value, approx=True)
+    return guess * (2.0 - value * guess)
+
+
 def law(strain, harden):
     volume = strain[0] + strain[1]
     normal = 0.5 * (strain[0] - strain[1])
     shear = 0.5 * strain[2]
     stiff = harden * (2.0 * normal * normal + 2.0 * shear * shear)
-    factor = (1.0 + 2.0 * stiff) / (1.0 + 3.0 * stiff)
+    factor = (1.0 + 2.0 * stiff) * inverse(1.0 + 3.0 * stiff)
     for turn in range(2):
         square = stiff * factor * factor
-        factor = (1.0 + 2.0 * square * factor) / (1.0 + 3.0 * square)
+        factor = (1.0 + 2.0 * square * factor) * inverse(1.0 + 3.0 * square)
     square = factor * factor
-    slope = -harden * square * factor / (1.0 + 3.0 * stiff * square)
+    slope = -harden * square * factor * inverse(1.0 + 3.0 * stiff * square)
     return volume, normal, shear, factor, slope
 
 
@@ -154,54 +159,65 @@
 
 def green(first, second, mixed, part_11, part_22, cross):
     across = cross * mixed
-    total = part_11 * first + 2.0 * across + part_22 * second
-    out_11 = (part_11 * first + across) * (1.0 / MU_REF) - COUPLE * part_11 * total
-    out_22 = (across + part_22 * second) * (1.0 / MU_REF) - COUPLE * part_22 * total
-    out_12 = (cross * (first + second) + (part_11 + part_22) * mixed) * (
-        1.0 / MU_REF
-    ) - 2.0 * COUPLE * cross * total
-    return out_11, out_22, out_12
+    one, two = part_11 * first + across, part_22 * second + across
+    total = (2.0 * MU_REF * COUPLE / 2.0) * (one + two)
+    return (
+        one - part_11 * total,
+        two - part_22 * total,
+        cross * (first + second - 2.0 * total) + (part_11 + part_22) * mixed,
+    )
 
 
 def kernel(
-    disp, body, assign, phase, flag, table_hbm,
-    correction_out, strain_out, hom_out,
-    table, pf, a1src, a1, nb, a2src, a2, c1src, c1, c2src, c2, d1src, d1, d2src, d2,
+    disp_hbm, body_hbm, assign_hbm, phase_hbm, flag_hbm,
+    correction_out, strain_0, strain_1, strain_2, hom_out,
+    disp, body, assign, table, pf, a1src, a1, nb, a2src, a2, c1src, c1, c2src, c2, d1src, d1, d2src, d2,
     halo_u, halo_f, halo_a,
     parts, labels, accs, green_tab, ph_f, hard_f, ind_h, mid_h, mid_l, spec, filt_h, filt_l,
     strains, last, basis, tangent,
-    sem_table, send, recv, gather_recv, halo_recv,
+    load, send, recv, gather_recv, halo_recv,
 ):
     r = lax.axis_index("rve")
     s = lax.axis_index("slab")
     y, core = s // 2, s % 2
     half, lane_field = s // 4, s % 4
     before, after = lax.rem(r + GROUPS - 1, GROUPS), lax.rem(r + 1, GROUPS)
+    peers = [(r, lax.rem(y + dy, 4) * 2 + (1 - core if dc else core)) for dy, dc in NEAR]
+    gx, gz = r // 8, r % 8
+    far = [(lax.rem(gx + dx, 4) * 8 + lax.rem(gz + dz, 8), s) for dx, dz in OFFSETS]
     left = (jnp.where(s == 0, before, r), lax.rem(s + SLABS - 1, SLABS))
     right = (jnp.where(s == SLABS - 1, after, r), lax.rem(s + 1, SLABS))
 
-    table_copy = pltpu.make_async_copy(table_hbm, table, sem_table)
-    table_copy.start()
+    loads = [
+        pltpu.make_async_copy(source, target, load.at[k])
+        for k, (source, target) in enumerate(
+            (
+                (disp_hbm, disp),
+                (assign_hbm, assign),
+                (phase_hbm.at[0], pf.at[core, y, 0]),
+                (flag_hbm.at[0], pf.at[core, y, 1]),
+                (body_hbm, body),
+            )
+        )
+    ]
+    for copy in loads:
+        copy.start()
 
     barrier = pltpu.get_barrier_semaphore()
 
     def greet(device):
         pl.semaphore_signal(barrier, inc=1, device_id=device, device_id_type=MESH)
 
-    for k in range(1, SLABS):
-        greet((r, lax.rem(s + k, SLABS)))
+    for device in far:
+        greet(device)
+    for device in peers:
+        greet(device)
     greet((after, 0))
 
     @pl.when(s == 0)
     def _():
         for k in range(SLABS):
             greet((before, k))
-
-    for k in range(1, GROUPS):
-        greet((lax.rem(r + k, GROUPS), s))
-
-    pf[core, y, 0] = phase[...]
-    pf[core, y, 1] = flag[...]
 
     def label_sums(rows, count):
         step = rows // 8
@@ -222,7 +238,7 @@
                 accs[c, label] = jnp.sum(sums[c].reshape(step, 8, 128), axis=0)
             return 0
 
-        lax.fori_loop(0, GROUPS, one, 0, unroll=4)
+        lax.fori_loop(0, GROUPS, one, 0, unroll=GROUPS if rows == 8 else 4)
         if not count:
             accs[3] = jnp.zeros((GROUPS, 8, 128), F32)
         folded = jnp.sum(accs[...].reshape(4 * GROUPS, 8, 128), axis=1)
@@ -238,6 +254,8 @@
             parts[k, 0:rows, :] = value
 
     row_of = lax.broadcasted_iota(jnp.int32, (BLOCK, 128), 0)
+    loads[0].wait()
+    loads[1].wait()
     own = [disp[0], disp[1]]
     beside = [jnp.where(row_of == BLOCK - 1, 0.0, columns_back(u)) for u in own]
     keep_parts(own + beside, BLOCK)
@@ -263,10 +281,14 @@
         green_tab[0, rows, :] = k1 * k1 * inverse
         green_tab[1, rows, :] = k2 * k2 * inverse
         green_tab[2, rows, :] = sign * k1 * k2 * inverse
+        table[0, rows, :], table[1, rows, :] = split(wave(row, lane))
+        table[2, rows, :], table[3, rows, :] = split(wave(lane, row))
         return 0
 
     lax.fori_loop(0, 8, symbols, 0)
 
+    for copy in loads[2:5]:
+        copy.wait()
     pl.semaphore_wait(barrier, SLABS - 1 + GROUPS - 1 + 1 + jnp.where(s == 0, SLABS, 0))
 
     def push(source, target, k, recv_sem, device):
@@ -277,8 +299,8 @@
     def drained(ref, sem):
         pltpu.make_async_copy(ref, ref, sem).wait()
 
-    for k in range(1, SLABS):
-        push(a1src, a1.at[s], 0, recv.at[0], (r, lax.rem(s + k, SLABS)))
+    for device in peers:
+        push(a1src, a1.at[s], 0, recv.at[0], device)
 
     @pl.when(s == 0)
     def _():
@@ -309,8 +331,8 @@
         labels[p, 0:8, :] = jnp.concatenate([gathered[k, 3 + p : 4 + p, :] for k in range(SLABS)], axis=0)
     a2src[...] = label_sums(8, False) + jnp.sum(gathered, axis=0)[0:1, :]
     a2[r] = a2src[...]
-    for k in range(1, GROUPS):
-        push(a2src, a2.at[r], 10, recv.at[3], (lax.rem(r + k, GROUPS), s))
+    for device in far:
+        push(a2src, a2.at[r], 10, recv.at[3], device)
 
     for k in range(1, 4):
         other = lax.rem(y + k, 4)
@@ -329,7 +351,6 @@
             ind_h[1, rows, :] = active.astype(BF16)
             ind_h[2, rows, :] = (here * active).astype(BF16)
 
-    table_copy.wait()
 
     def along_x(high, low, rows=slice(None), which=0):
         left_h, left_l = table[which, rows, :], table[which + 1, rows, :]
@@ -360,7 +381,9 @@
         bulk, modulus = (6.0, 3.0) if p else (2.0, 1.0)
         for f in range(2):
             state = law(mean, (0.5 if p else 2.0) * f)
-            kinds[p, f] = stress_of(state, bulk, modulus) + image_of(state, bulk, modulus, units)
+            kinds[p, f] = stress_of(state, bulk / MU_REF, modulus / MU_REF) + image_of(
+                state, bulk / MU_REF, modulus / MU_REF, units
+            )
     weights = []
     for k in range(6):
         base = kinds[0, 0][k]
@@ -387,7 +410,7 @@
                             filt_l[3 * n + c, rr, ll] = low
             return 0
 
-        lax.fori_loop(0, 8, rows_of, 0)
+        lax.fori_loop(0, 8, rows_of, 0, unroll=4)
 
     def wide(value):
         return jnp.concatenate([value, value], axis=0)
@@ -417,7 +440,7 @@
             lanes = slice(b * HALF, (b + 1) * HALF)
             here = ph_f[rows, lanes]
             state = law([strains[c, rows, lanes] for c in range(3)], hard_f[rows, lanes])
-            bulk, modulus = 2.0 + 4.0 * here, 1.0 + 2.0 * here
+            bulk, modulus = 1.0 + 2.0 * here, 0.5 + here
             values = stress_of(state, bulk, modulus) + image_of(
                 state, bulk, modulus, [strains[3 + c, rows, lanes] for c in range(3)]
             )
@@ -425,7 +448,7 @@
                 filt_h[c, rows, lanes], filt_l[c, rows, lanes] = split(values[c])
         return 0
 
-    lax.fori_loop(0, 16, material, 0)
+    lax.fori_loop(0, 16, material, 0, unroll=4)
     for k in range(6):
         mid_h[k], mid_l[k] = split(along_y(filt_h[k], filt_l[k], 2))
     for k in range(6):
@@ -460,8 +483,9 @@
                 sums[c] = sums[c] + values[c][0:8, :] + values[c][8:16, :]
         return tuple(sums)
 
-    sums = lax.fori_loop(0, 8, finish, tuple(jnp.zeros((8, 128), F32) for c in range(6)))
-    strain_out[0] = last[0:3, pl.ds(pl.multiple_of(lane_field * BLOCK, BLOCK), BLOCK), :]
+    sums = lax.fori_loop(0, 8, finish, tuple(jnp.zeros((8, 128), F32) for c in range(6)), unroll=4)
+    for c, strain_out in enumerate((strain_0, strain_1, strain_2)):
+        strain_out[...] = last[c, pl.ds(pl.multiple_of(lane_field * BLOCK, BLOCK), BLOCK), :]
 
     message = jnp.zeros((1, 128), F32)
     for c in range(3):
@@ -474,8 +498,8 @@
         message = message + jnp.where((lane1 == 12 + c) & (s == 0), mean[c][0:1, :], 0.0)
     c1src[...] = message
     c1[s] = message
-    for k in range(1, SLABS):
-        push(c1src, c1.at[s], 11, recv.at[4], (r, lax.rem(s + k, SLABS)))
+    for device in peers:
+        push(c1src, c1.at[s], 11, recv.at[4], device)
 
     for k, halo in enumerate((halo_u, halo_f, halo_a)):
         drained(halo.at[0], halo_recv.at[k, 0])
@@ -494,8 +518,8 @@
     drained(c1.at[pl.ds(0, SLABS - 1)], recv.at[4])
     c2src[...] = jnp.sum(c1[...], axis=0)
     c2[r] = c2src[...]
-    for k in range(1, GROUPS):
-        push(c2src, c2.at[r], 12, recv.at[5], (lax.rem(r + k, GROUPS), s))
+    for device in far:
+        push(c2src, c2.at[r], 12, recv.at[5], device)
     drained(c2.at[pl.ds(0, GROUPS - 1)], recv.at[5])
     square = jnp.concatenate([c2[...].reshape(GROUPS, 128), jnp.zeros((128 - GROUPS, 128), F32)], axis=0)
     by_label = square.T[0:16, :]
@@ -561,13 +585,13 @@
     diagonal = lax.broadcasted_iota(jnp.int32, (16, 128), 0) == lane_iota((16, 128))
     d1src[...] = jnp.sum(jnp.where(diagonal, stacked, 0.0), axis=0, keepdims=True)
     d1[s] = d1src[...]
-    for k in range(1, SLABS):
-        push(d1src, d1.at[s], 13, recv.at[6], (r, lax.rem(s + k, SLABS)))
+    for device in peers:
+        push(d1src, d1.at[s], 13, recv.at[6], device)
     drained(d1.at[pl.ds(0, SLABS - 1)], recv.at[6])
     d2src[...] = jnp.sum(d1[...], axis=0)
     d2[r] = d2src[...]
-    for k in range(1, GROUPS):
-        push(d2src, d2.at[r], 14, recv.at[7], (lax.rem(r + k, GROUPS), s))
+    for device in far:
+        push(d2src, d2.at[r], 14, recv.at[7], device)
     drained(d2.at[pl.ds(0, GROUPS - 1)], recv.at[7])
     gram_row = jnp.sum(d2[...], axis=0)
     gram = {}
@@ -631,22 +655,61 @@
     drained(d2.at[pl.ds(0, GROUPS - 1)], send.at[14])
 
 
-def shards(displacement, body_force, assignment, phases, flags):
-    tables = jnp.asarray(transform_tables())
-    vmem = pl.BlockSpec(memory_space=pltpu.VMEM)
-    row = lambda n: pltpu.VMEM((n, 1, 128), F32)
-    one_row = pltpu.VMEM((1, 128), F32)
-    square = (GRID, GRID)
-    correction, strain, hom = pl.pallas_call(
-        kernel,
+def write_kernel(one, two_a, two_b, two_c, three, one_out, two_out, three_out, sems):
+    copies = [
+        pltpu.make_async_copy(source, target, sems.at[k])
+        for k, (source, target) in enumerate(
+            (
+                (one, one_out),
+                (two_a, two_out.at[0, 0]),
+                (two_b, two_out.at[0, 1]),
+                (two_c, two_out.at[0, 2]),
+                (three, three_out),
+            )
+        )
+    ]
+    for copy in copies:
+        copy.start()
+    for copy in copies:
+        copy.wait()
+
+
+def written(*values):
+    return pl.pallas_call(
+        write_kernel,
         out_shape=(
             jax.ShapeDtypeStruct((2, BLOCK, 128), F32),
             jax.ShapeDtypeStruct((1, 3, BLOCK, GRID), F32),
             jax.ShapeDtypeStruct((12, GROUPS), F32),
         ),
-        in_specs=[vmem] * 5 + [pl.BlockSpec(memory_space=pl.ANY)],
-        out_specs=(vmem, vmem, vmem),
+        in_specs=[pl.BlockSpec(memory_space=pl.ANY)] * 5,
+        out_specs=(pl.BlockSpec(memory_space=pltpu.HBM),) * 3,
+        scratch_shapes=[pltpu.SemaphoreType.DMA((5,))],
+        compiler_params=pltpu.CompilerParams(vmem_limit_bytes=4 * 1024 * 1024),
+        name="write_out",
+    )(*values)
+
+
+def shards(displacement, body_force, assignment, phases, flags):
+    vmem = pl.BlockSpec(memory_space=pltpu.VMEM)
+    row = lambda n: pltpu.VMEM((n, 1, 128), F32)
+    one_row = pltpu.VMEM((1, 128), F32)
+    square = (GRID, GRID)
+    results = pl.pallas_call(
+        kernel,
+        out_shape=(
+            jax.ShapeDtypeStruct((2, BLOCK, 128), F32),
+            jax.ShapeDtypeStruct((BLOCK, GRID), F32),
+            jax.ShapeDtypeStruct((BLOCK, GRID), F32),
+            jax.ShapeDtypeStruct((BLOCK, GRID), F32),
+            jax.ShapeDtypeStruct((12, GROUPS), F32),
+        ),
+        in_specs=[pl.BlockSpec(memory_space=pltpu.HBM)] * 5,
+        out_specs=(vmem,) * 5,
         scratch_shapes=[
+            pltpu.VMEM((2, BLOCK, 128), F32),
+            pltpu.VMEM((2, BLOCK, 128), F32),
+            pltpu.VMEM((4, BLOCK, 128), jnp.int32),
             pltpu.VMEM((4,) + square, BF16),
             pltpu.VMEM((2, 4, 2, BLOCK, GRID), jnp.int32),
             pltpu.VMEM((8, 128), F32),
@@ -673,18 +736,18 @@
             pltpu.VMEM((6, HALF, GRID), F32),
             pltpu.VMEM((CG_STEPS + 1, 2, BLOCK, 128), F32),
             pltpu.VMEM((4, 9, EXT, 128), F32),
-            pltpu.SemaphoreType.DMA,
+            pltpu.SemaphoreType.DMA((5,)),
             pltpu.SemaphoreType.DMA((15,)),
             pltpu.SemaphoreType.DMA((8,)),
             pltpu.SemaphoreType.DMA((4,)),
             pltpu.SemaphoreType.DMA((3, 2)),
         ],
         compiler_params=pltpu.CompilerParams(
-            collective_id=0, has_side_effects=True, vmem_limit_bytes=48 * 1024 * 1024
+            collective_id=0, has_side_effects=True, vmem_limit_bytes=55080 * 1024
         ),
         name="fe2_step",
-    )(displacement, body_force, assignment, phases[0], flags[0], tables)
-    return correction, strain, hom
+    )(displacement, body_force, assignment, phases, flags)
+    return written(*results)
 
 
 def solution(mesh):

time: 57.3 us -> 50.9 us (0.89)
  local copies, waits for them, and re-layouts: 6.76 us -> 0 us
  Pallas kernels: 49.5 us -> 50.1 us
    unnamed x15 -> x0, local copies, waits for them, and re-layouts: 6.76 us -> none
    pallas_call x0 -> x1, Pallas kernels: none -> 0.7 us  [written(): pl.pallas_call(write_kernel, out_shape=(jax.ShapeDtypeStruct((2, BLOCK, 1...]
where the time goes in v2:
time: 50.9 us; the launch traced here: 50.8 us
  Pallas kernels  50.1 us (98%)
  between operations  0.64 us (1%)
    pallas_call x1, Pallas kernels, shards(): pl.pallas_call(kernel, out_shape=(jax.ShapeDtypeStruct((2, BLOCK, 128), F...  49.4 us

profile of v2, /device:TPU:1, one launch (start us, length us, event | category | flops | bytes accessed | tf_op | source)
XLA Modules:
  0.0 50.8 jit_solution(6154684539597031158)
XLA Ops:
  0.6 49.4 %fe2_step.1 = (f32[2,32,128]{2,1,0:T(8,128)S(1)}, f32[32,256]{1,0:T(8,128)S(1)}, f32[32,256]{1,0:T(8,128)S(1)}, f32[32,256]{1,0:T(8,128)S(1)}, f32[12,32]{1,0:T(8,128)S(1)}) custom-call(f32[2,32,128]{2,1,0:T(8,128)} %disp_hbm.1, f32[2,32,128]{2,1,0:T(8,128)} %body_hbm.1, s32[4,32,128]{2,1,0:T(8,128)} %assign_hbm.1, s32[1,32,256]{2,1,0:T(8,128)} %phase_hbm.1, ...), custom_call_target="tpu_custom_call" | custom-call | tf_op jit(solution)/shard_map/fe2_step/pallas_call | solution.py:698
  50.1 0.7 %write_out.1 = (f32[2,32,128]{2,1,0:T(8,128)}, f32[1,3,32,256]{3,2,1,0:T(8,128)}, f32[12,32]{1,0:T(8,128)}) custom-call(f32[2,32,128]{2,1,0:T(8,128)S(1)} %get-tuple-element.8.one, f32[32,256]{1,0:T(8,128)S(1)} %get-tuple-element.9.two_a, f32[32,256]{1,0:T(8,128)S(1)} %get-tuple-element.10.two_b, f32[32,256]{1,0:T(8,128)S(1)} %get-tuple-element.11.two_c, ...), custom_call_target="tpu_custom_call" | custom-call | tf_op jit(solution)/shard_map/write_out/pallas_call | solution.py:678

commit v3 on v2

--- a/solution.py
+++ b/solution.py
@@ -86,17 +86,35 @@
 
 
 def strain_parts(first, second, first_next, second_next):
-    across_1 = first_next - first
-    across_2 = second_next - second
-    across_1_up, across_2_up = rows_up(across_1), rows_up(across_2)
-    up_1, up_2 = rows_up(first) - first, rows_up(second) - second
-    up_1_next = rows_up(first_next) - first_next
-    up_2_next = rows_up(second_next) - second_next
-    d1x = [(1.0 - t) * across_1 + t * across_1_up for t in ENDS]
-    d2x = [(1.0 - t) * across_2 + t * across_2_up for t in ENDS]
-    d1y = [(1.0 - s) * up_1 + s * up_1_next for s in ENDS]
-    d2y = [(1.0 - s) * up_2 + s * up_2_next for s in ENDS]
-    return d1x, d2y, d1y, d2x
+    slopes = []
+    for here, beside in ((first, first_next), (second, second_next)):
+        above = rows_up(here)
+        both = rows_up(beside)
+        across, across_up = beside - here, both - above
+        up, up_next = above - here, both - beside
+        slopes.append(
+            (
+                [(1.0 - t) * across + t * across_up for t in ENDS],
+                [(1.0 - s) * up + s * up_next for s in ENDS],
+            )
+        )
+    return slopes[0][0], slopes[1][1], slopes[0][1], slopes[1][0]
+
+
+def strain_parts_ext(field):
+    slopes = []
+    for here in field:
+        above = rows_up(here)
+        beside, both = columns_back(here), columns_back(above)
+        across, across_up = beside - here, both - above
+        up, up_next = above - here, both - beside
+        slopes.append(
+            (
+                [(1.0 - t) * across + t * across_up for t in ENDS],
+                [(1.0 - s) * up + s * up_next for s in ENDS],
+            )
+        )
+    return slopes[0][0], slopes[1][1], slopes[0][1], slopes[1][0]
 
 
 def assemble(stress):
@@ -110,11 +128,10 @@
 
     forces = []
     for normal_x, normal_y in ((0, 2), (2, 1)):
-        low, high = mixed([by_t(normal_x, t) for t in range(2)])
-        over_x = low + rows_down(high)
-        low, high = mixed([by_s(normal_y, s) for s in range(2)])
-        over_y = low + columns_on(high)
-        forces.append(columns_on(over_x) - over_x + rows_down(over_y) - over_y)
+        low_x, high_x = mixed([by_t(normal_x, t) for t in range(2)])
+        low_y, high_y = mixed([by_s(normal_y, s) for s in range(2)])
+        on = low_x - high_y + rows_down(high_x + high_y)
+        forces.append(columns_on(on) - (low_x + low_y) + rows_down(low_y - high_x))
     return forces
 
 
@@ -173,7 +190,7 @@
     correction_out, strain_0, strain_1, strain_2, hom_out,
     disp, body, assign, table, pf, a1src, a1, nb, a2src, a2, c1src, c1, c2src, c2, d1src, d1, d2src, d2,
     halo_u, halo_f, halo_a,
-    parts, labels, accs, green_tab, ph_f, hard_f, ind_h, mid_h, mid_l, spec, filt_h, filt_l,
+    parts, labels, accs, green_tab, ph_f, hard_f, mid_h, mid_l, spec, filt_h, filt_l,
     strains, last, basis, tangent,
     load, send, recv, gather_recv, halo_recv,
 ):
@@ -208,16 +225,17 @@
     def greet(device):
         pl.semaphore_signal(barrier, inc=1, device_id=device, device_id_type=MESH)
 
+    greet((after, 0))
+
+    @pl.when(s == 0)
+    def _():
+        for k in range(SLABS):
+            greet((before, k))
+
     for device in far:
         greet(device)
     for device in peers:
         greet(device)
-    greet((after, 0))
-
-    @pl.when(s == 0)
-    def _():
-        for k in range(SLABS):
-            greet((before, k))
 
     def label_sums(rows, count):
         step = rows // 8
@@ -299,13 +317,13 @@
     def drained(ref, sem):
         pltpu.make_async_copy(ref, ref, sem).wait()
 
-    for device in peers:
-        push(a1src, a1.at[s], 0, recv.at[0], device)
-
     @pl.when(s == 0)
     def _():
         for k in range(SLABS):
             push(a1src, nb, 1, recv.at[1], (before, k))
+
+    for device in peers:
+        push(a1src, a1.at[s], 0, recv.at[0], device)
 
     sibling = (r, y * 2 + 1 - core)
     for k in range(1, 4):
@@ -334,23 +352,29 @@
     for device in far:
         push(a2src, a2.at[r], 10, recv.at[3], device)
 
+    def take_block(slab, chip):
+        rows = pl.ds(pl.multiple_of((chip * 2 + slab) * BLOCK, BLOCK), BLOCK)
+        here = pf[slab, chip, 0].astype(F32)
+        active = pf[slab, chip, 1].astype(F32)
+        ph_f[rows, :] = here
+        hard_f[rows, :] = active * (2.0 - 1.5 * here)
+        kinds_of = [here.astype(BF16), active.astype(BF16), (here * active).astype(BF16)]
+        block = jnp.concatenate(kinds_of, axis=0)
+        value = dot(block, table[2]) + dot(block, table[3])
+        for m in range(3):
+            part_h, part_l = split(value[m * BLOCK : (m + 1) * BLOCK])
+            mid_h[m, rows, :] = part_h
+            mid_l[m, rows, :] = part_l
+
+    take_block(core, y)
     for k in range(1, 4):
         other = lax.rem(y + k, 4)
         drained(pf.at[core, other], gather_recv.at[other])
         push(pf.at[core, other], pf.at[core, other], 3, recv.at[2], sibling)
+        take_block(core, other)
     drained(pf.at[1 - core], recv.at[2])
-
-    for yy in range(4):
-        for cc in range(2):
-            rows = slice((yy * 2 + cc) * BLOCK, (yy * 2 + cc + 1) * BLOCK)
-            here = pf[cc, yy, 0].astype(F32)
-            active = pf[cc, yy, 1].astype(F32)
-            ph_f[rows, :] = here
-            hard_f[rows, :] = active * (2.0 - 1.5 * here)
-            ind_h[0, rows, :] = here.astype(BF16)
-            ind_h[1, rows, :] = active.astype(BF16)
-            ind_h[2, rows, :] = (here * active).astype(BF16)
-
+    for k in range(4):
+        take_block(1 - core, k)
 
     def along_x(high, low, rows=slice(None), which=0):
         left_h, left_l = table[which, rows, :], table[which + 1, rows, :]
@@ -360,9 +384,6 @@
         right_h, right_l = table[which], table[which + 1]
         return dot(high, right_h) + dot(high, right_l) + dot(low, right_h)
 
-    for m in range(3):
-        value = dot(ind_h[m], table[2]) + dot(ind_h[m], table[3])
-        mid_h[m], mid_l[m] = split(value)
     for m in range(3):
         spec[m] = along_x(mid_h[m], mid_l[m])
 
@@ -391,51 +412,59 @@
         by_flag = kinds[0, 1][k] - base
         weights.append((by_phase, by_flag, kinds[1, 1][k] - base - by_phase - by_flag))
 
-    def filter_all(load):
-        def rows_of(k, _):
+    def filter_pieces(load, n):
+        def piece(k):
             for a in range(2):
-                rows = pl.ds(pl.multiple_of(a * HALF + k * 16, 16), 16)
-                swap_rows = pl.ds(pl.multiple_of((1 - a) * HALF + k * 16, 16), 16)
+                rows = slice(a * HALF + k * 16, a * HALF + k * 16 + 16)
+                swap_rows = slice((1 - a) * HALF + k * 16, (1 - a) * HALF + k * 16 + 16)
                 for b in range(2):
                     lanes = slice(b * HALF, (b + 1) * HALF)
                     swap_lanes = slice((1 - b) * HALF, (2 - b) * HALF)
                     sym = [green_tab[i, rows, lanes] for i in range(3)]
-                    firsts, seconds, mixeds = load(rows, lanes, swap_rows, swap_lanes)
-                    for n in range(2):
-                        out = green(firsts[n], seconds[n], mixeds[n], *sym)
-                        for c in range(3):
-                            rr, ll = (swap_rows, swap_lanes) if c == 2 else (rows, lanes)
-                            high, low = split(out[c])
-                            filt_h[3 * n + c, rr, ll] = high
-                            filt_l[3 * n + c, rr, ll] = low
-            return 0
-
-        lax.fori_loop(0, 8, rows_of, 0, unroll=4)
+                    out = green(*load(n, rows, lanes, swap_rows, swap_lanes), *sym)
+                    for c in range(3):
+                        rr, ll = (swap_rows, swap_lanes) if c == 2 else (rows, lanes)
+                        high, low = split(out[c])
+                        filt_h[3 * n + c, rr, ll] = high
+                        filt_l[3 * n + c, rr, ll] = low
+
+        return [lambda k=k: piece(k) for k in range(8)]
+
+    def together(first, second):
+        turns = max(len(first), len(second))
+        for k in range(turns):
+            for pieces in (first, second):
+                for j in range(k * len(pieces) // turns, (k + 1) * len(pieces) // turns):
+                    pieces[j]()
 
     def wide(value):
         return jnp.concatenate([value, value], axis=0)
 
     wide_weights = [[wide(w) for w in three] for three in weights]
 
-    def load_first(rows, lanes, swap_rows, swap_lanes):
+    def load_first(n, rows, lanes, swap_rows, swap_lanes):
         here = [spec[m, rows, lanes] for m in range(3)]
         there = [spec[m, swap_rows, swap_lanes] for m in range(3)]
         mix = lambda k, fields: sum(wide_weights[k][m] * fields[m] for m in range(3))
-        return (
-            [mix(0, here), mix(3, here)],
-            [mix(1, here), mix(4, here)],
-            [mix(2, there), mix(5, there)],
-        )
-
-    filter_all(load_first)
+        return mix(3 * n, here), mix(3 * n + 1, here), mix(3 * n + 2, there)
 
     start = mean + units
-    for k in range(6):
-        high, low = split(along_x(filt_h[k], filt_l[k], which=2))
-        strains[k] = jnp.broadcast_to(start[k][0:1, 0:1], (GRID, GRID)) - along_y(high, low, 0)
-
-    def material(k, _):
-        rows = pl.ds(pl.multiple_of(k * 16, 16), 16)
+
+    def invert_first(n):
+        def one(k):
+            high, low = split(along_x(filt_h[k], filt_l[k], which=2))
+            strains[k] = jnp.broadcast_to(start[k][0:1, 0:1], (GRID, GRID)) - along_y(high, low, 0)
+
+        return [lambda k=k: one(k) for k in range(3 * n, 3 * n + 3)]
+
+    for piece in filter_pieces(load_first, 0):
+        piece()
+    together(filter_pieces(load_first, 1), invert_first(0))
+    for piece in invert_first(1):
+        piece()
+
+    def material(k):
+        rows = slice(k * 16, k * 16 + 16)
         for b in range(2):
             lanes = slice(b * HALF, (b + 1) * HALF)
             here = ph_f[rows, lanes]
@@ -446,26 +475,43 @@
             )
             for c in range(6):
                 filt_h[c, rows, lanes], filt_l[c, rows, lanes] = split(values[c])
-        return 0
-
-    lax.fori_loop(0, 16, material, 0, unroll=4)
-    for k in range(6):
-        mid_h[k], mid_l[k] = split(along_y(filt_h[k], filt_l[k], 2))
-    for k in range(6):
-        spec[k] = along_x(mid_h[k], mid_l[k])
-
-    def load_second(rows, lanes, swap_rows, swap_lanes):
-        return (
-            [spec[0, rows, lanes], spec[3, rows, lanes]],
-            [spec[1, rows, lanes], spec[4, rows, lanes]],
-            [spec[2, swap_rows, swap_lanes], spec[5, swap_rows, swap_lanes]],
-        )
-
-    filter_all(load_second)
+
+    def forward_y(q):
+        rows = slice(q * 64, q * 64 + 64)
+        stacked = lambda ref: jnp.concatenate([ref[c, rows, :] for c in range(6)], axis=0)
+        high, low = split(along_y(stacked(filt_h), stacked(filt_l), 2))
+        for c in range(6):
+            mid_h[c, rows, :] = high[c * 64 : c * 64 + 64]
+            mid_l[c, rows, :] = low[c * 64 : c * 64 + 64]
+
+    for q in range(5):
+        pieces = [lambda k=k: material(k) for k in range(4 * q, 4 * q + 4)] if q < 4 else []
+        together(pieces, [lambda: forward_y(q - 1)] if q else [])
+
+    def load_second(n, rows, lanes, swap_rows, swap_lanes):
+        return spec[3 * n, rows, lanes], spec[3 * n + 1, rows, lanes], spec[3 * n + 2, swap_rows, swap_lanes]
+
     part = pl.ds(pl.multiple_of(half * HALF, HALF), HALF)
-    for k in range(6):
-        high, low = split(along_x(filt_h[k], filt_l[k], rows=part, which=2))
-        last[k] = strains[k, part, :] - along_y(high, low, 0)
+
+    def forward_x(n):
+        def one(k):
+            spec[k] = along_x(mid_h[k], mid_l[k])
+
+        return [lambda k=k: one(k) for k in range(3 * n, 3 * n + 3)]
+
+    def invert_second(n):
+        def one(k):
+            high, low = split(along_x(filt_h[k], filt_l[k], rows=part, which=2))
+            last[k] = strains[k, part, :] - along_y(high, low, 0)
+
+        return [lambda k=k: one(k) for k in range(3 * n, 3 * n + 3)]
+
+    for piece in forward_x(0):
+        piece()
+    together(filter_pieces(load_second, 0), forward_x(1))
+    together(filter_pieces(load_second, 1), invert_second(0))
+    for piece in invert_second(1):
+        piece()
 
     def finish(k, sums):
         rows = pl.ds(pl.multiple_of(k * 16, 16), 16)
@@ -513,7 +559,7 @@
     u = [jnp.where(inside, extended(halo_u, disp, c), 0.0) for c in range(2)]
     force = [extended(halo_f, body, c) for c in range(2)]
     index = [jnp.where(inside, extended(halo_a, assign, p), 127) for p in range(4)]
-    u_parts = strain_parts(u[0], u[1], columns_back(u[0]), columns_back(u[1]))
+    u_parts = strain_parts_ext(u)
 
     drained(c1.at[pl.ds(0, SLABS - 1)], recv.at[4])
     c2src[...] = jnp.sum(c1[...], axis=0)
@@ -556,7 +602,7 @@
     basis[0, 0], basis[0, 1] = vector[0][8:40], vector[1][8:40]
 
     def stiffness(field):
-        shapes = strain_parts(field[0], field[1], columns_back(field[0]), columns_back(field[1]))
+        shapes = strain_parts_ext(field)
         result = []
         for p in range(4):
             strain = point_strain(shapes, p)
@@ -726,7 +772,6 @@
             pltpu.VMEM((3,) + square, F32),
             pltpu.VMEM(square, F32),
             pltpu.VMEM(square, F32),
-            pltpu.VMEM((3,) + square, BF16),
             pltpu.VMEM((6,) + square, BF16),
             pltpu.VMEM((6,) + square, BF16),
             pltpu.VMEM((6,) + square, F32),

time: 50.9 us -> 48.8 us (0.959)
  Pallas kernels: 50.1 us -> 48 us
    pallas_call x1, Pallas kernels: 49.4 us -> 47.3 us  [shards(): pl.pallas_call(kernel, out_shape=(jax.ShapeDtypeStruct((2, BLOCK, 128), F...]
where the time goes in v3:
time: 48.8 us; the launch traced here: 48.6 us
  Pallas kernels  48 us (98%)
  between operations  0.64 us (1%)
    pallas_call x1, Pallas kernels, shards(): pl.pallas_call(kernel, out_shape=(jax.ShapeDtypeStruct((2, BLOCK, 128), F...  47.3 us

profile of v3, /device:TPU:1, one launch (start us, length us, event | category | flops | bytes accessed | tf_op | source)
XLA Modules:
  0.0 48.6 jit_solution(17506003480694356018)
XLA Ops:
  0.6 47.3 %fe2_step.1 = (f32[2,32,128]{2,1,0:T(8,128)S(1)}, f32[32,256]{1,0:T(8,128)S(1)}, f32[32,256]{1,0:T(8,128)S(1)}, f32[32,256]{1,0:T(8,128)S(1)}, f32[12,32]{1,0:T(8,128)S(1)}) custom-call(f32[2,32,128]{2,1,0:T(8,128)} %disp_hbm.1, f32[2,32,128]{2,1,0:T(8,128)} %body_hbm.1, s32[4,32,128]{2,1,0:T(8,128)} %assign_hbm.1, s32[1,32,256]{2,1,0:T(8,128)} %phase_hbm.1, ...), custom_call_target="tpu_custom_call" | custom-call | tf_op jit(solution)/shard_map/fe2_step/pallas_call | solution.py:744
  47.9 0.7 %write_out.1 = (f32[2,32,128]{2,1,0:T(8,128)}, f32[1,3,32,256]{3,2,1,0:T(8,128)}, f32[12,32]{1,0:T(8,128)}) custom-call(f32[2,32,128]{2,1,0:T(8,128)S(1)} %get-tuple-element.8.one, f32[32,256]{1,0:T(8,128)S(1)} %get-tuple-element.9.two_a, f32[32,256]{1,0:T(8,128)S(1)} %get-tuple-element.10.two_b, f32[32,256]{1,0:T(8,128)S(1)} %get-tuple-element.11.two_c, ...), custom_call_target="tpu_custom_call" | custom-call | tf_op jit(solution)/shard_map/write_out/pallas_call | solution.py:724

commit v4 on v3

--- a/solution.py
+++ b/solution.py
@@ -192,7 +192,7 @@
     halo_u, halo_f, halo_a,
     parts, labels, accs, green_tab, ph_f, hard_f, mid_h, mid_l, spec, filt_h, filt_l,
     strains, last, basis, tangent,
-    load, send, recv, gather_recv, halo_recv,
+    relay, load, send, recv, gather_recv, halo_recv,
 ):
     r = lax.axis_index("rve")
     s = lax.axis_index("slab")
@@ -225,16 +225,29 @@
     def greet(device):
         pl.semaphore_signal(barrier, inc=1, device_id=device, device_id_type=MESH)
 
-    greet((after, 0))
-
-    @pl.when(s == 0)
-    def _():
-        for k in range(SLABS):
+    ring_z = {dz: (gx * 8 + lax.rem(gz + dz, 8), s) for dz in (1, 2, 6, 7)}
+    ring_x = [(lax.rem(gx + dx, 4) * 8 + gz, s) for dx in (2, 1, 3)]
+    opposite = y == 2
+    across = (jnp.where(opposite, before, after), jnp.where(opposite, SLABS - 1, 0))
+    has_across = jnp.where(opposite, r > 0, r < GROUPS - 1)
+    gives_back, gives_on = (s == 0) & (r > 0), (s == SLABS - 1) & (r < GROUPS - 1)
+    has_left, has_right = (s > 0) | (r > 0), (s < SLABS - 1) | (r < GROUPS - 1)
+
+    @pl.when(has_across)
+    def _():
+        greet(across)
+
+    @pl.when(gives_back)
+    def _():
+        for k in (0, 1, 2, 3, 6, 7):
             greet((before, k))
 
-    for device in far:
-        greet(device)
-    for device in peers:
+    @pl.when(gives_on)
+    def _():
+        for k in (4, 5):
+            greet((after, k))
+
+    for device in [ring_z[2], ring_z[6]] + ring_x + peers + [ring_z[1], ring_z[7]]:
         greet(device)
 
     def label_sums(rows, count):
@@ -257,14 +270,19 @@
             return 0
 
         lax.fori_loop(0, GROUPS, one, 0, unroll=GROUPS if rows == 8 else 4)
+        used = 4 if count else 3
+        folded = jnp.sum(accs[0:used].reshape(used * GROUPS, 8, 128), axis=1)
         if not count:
-            accs[3] = jnp.zeros((GROUPS, 8, 128), F32)
-        folded = jnp.sum(accs[...].reshape(4 * GROUPS, 8, 128), axis=1)
-        ones = jnp.ones((8, 128), F32)
-        return lax.dot_general(
-            ones, folded, (((1,), (1,)), ((), ())),
-            precision=lax.Precision.HIGHEST, preferred_element_type=F32,
-        )[0:1, :]
+            folded = jnp.concatenate([folded, jnp.zeros((GROUPS, 128), F32)], axis=0)
+        ones = jnp.ones((8, 128), BF16)
+        total = jnp.zeros((8, 128), F32)
+        for turn in range(3):
+            piece = folded.astype(BF16)
+            folded = folded - piece.astype(F32)
+            total = total + lax.dot_general(
+                ones, piece, (((1,), (1,)), ((), ())), preferred_element_type=F32
+            )
+        return total[0:1, :]
 
     def keep_parts(fields, rows):
         d1x, d2y, d1y, d2x = strain_parts(*fields)
@@ -287,6 +305,56 @@
     )
     a1[s] = a1src[...]
 
+    for copy in loads[2:5]:
+        copy.wait()
+    pl.semaphore_wait(
+        barrier,
+        SLABS - 1 + 3 + 4 + jnp.where(has_across, 1, 0) + jnp.where(gives_back, 6, 0) + jnp.where(gives_on, 2, 0),
+    )
+
+    def push(source, target, k, recv_sem, device):
+        pltpu.make_async_remote_copy(
+            source, target, send.at[k], recv_sem, device_id=device, device_id_type=MESH
+        ).start()
+
+    def drained(ref, sem):
+        pltpu.make_async_copy(ref, ref, sem).wait()
+
+    @pl.when(gives_back)
+    def _():
+        for k in (0, 1, 2, 3, 6, 7):
+            push(a1src, nb, 1, recv.at[1], (before, k))
+
+    @pl.when(gives_on)
+    def _():
+        for k in (4, 5):
+            push(a1src, nb, 1, recv.at[1], (after, k))
+
+    for device in peers:
+        push(a1src, a1.at[s], 0, recv.at[0], device)
+
+    sibling = (r, y * 2 + 1 - core)
+    for k in range(1, 4):
+        push(pf.at[core, y], pf.at[core, y], 2, gather_recv.at[y], (r, lax.rem(y + k, 4) * 2 + core))
+    push(pf.at[core, y], pf.at[core, y], 3, recv.at[2], sibling)
+
+    strip = ((disp, halo_u), (body, halo_f), (assign, halo_a))
+
+    @pl.when(has_left)
+    def _():
+        for k, (own_ref, halo) in enumerate(strip):
+            push(own_ref.at[:, pl.ds(0, 8), :], halo.at[1], 4 + 2 * k, halo_recv.at[k, 1], left)
+
+    @pl.when(has_right)
+    def _():
+        for k, (own_ref, halo) in enumerate(strip):
+            push(own_ref.at[:, pl.ds(BLOCK - 8, 8), :], halo.at[0], 5 + 2 * k, halo_recv.at[k, 0], right)
+
+    def tell(k, devices):
+        for device in devices:
+            pl.semaphore_signal(relay.at[k], inc=1, device_id=device, device_id_type=MESH)
+
+    tell(0, [ring_z[2], ring_z[6]])
     def symbols(k, _):
         rows = pl.ds(pl.multiple_of(k * 32, 32), 32)
         row = lax.broadcasted_iota(jnp.int32, (32, GRID), 0) + k * 32
@@ -305,50 +373,36 @@
 
     lax.fori_loop(0, 8, symbols, 0)
 
-    for copy in loads[2:5]:
-        copy.wait()
-    pl.semaphore_wait(barrier, SLABS - 1 + GROUPS - 1 + 1 + jnp.where(s == 0, SLABS, 0))
-
-    def push(source, target, k, recv_sem, device):
-        pltpu.make_async_remote_copy(
-            source, target, send.at[k], recv_sem, device_id=device, device_id_type=MESH
-        ).start()
-
-    def drained(ref, sem):
-        pltpu.make_async_copy(ref, ref, sem).wait()
-
-    @pl.when(s == 0)
-    def _():
-        for k in range(SLABS):
-            push(a1src, nb, 1, recv.at[1], (before, k))
-
-    for device in peers:
-        push(a1src, a1.at[s], 0, recv.at[0], device)
-
-    sibling = (r, y * 2 + 1 - core)
-    for k in range(1, 4):
-        push(pf.at[core, y], pf.at[core, y], 2, gather_recv.at[y], (r, lax.rem(y + k, 4) * 2 + core))
-    push(pf.at[core, y], pf.at[core, y], 3, recv.at[2], sibling)
-
-    for k, (own_ref, halo) in enumerate(((disp, halo_u), (body, halo_f), (assign, halo_a))):
-        push(own_ref.at[:, pl.ds(0, 8), :], halo.at[1], 4 + 2 * k, halo_recv.at[k, 1], left)
-        push(own_ref.at[:, pl.ds(BLOCK - 8, 8), :], halo.at[0], 5 + 2 * k, halo_recv.at[k, 0], right)
+    pl.semaphore_wait(relay.at[0], 2)
+    tell(1, ring_x)
 
     drained(a1.at[pl.ds(0, SLABS - 1)], recv.at[0])
-    drained(nb, recv.at[1])
+    @pl.when(has_across)
+    def _():
+        drained(nb, recv.at[1])
+
+    @pl.when(jnp.logical_not(has_across))
+    def _():
+        nb[...] = jnp.zeros((8, 128), F32)
+
     row8 = lax.broadcasted_iota(jnp.int32, (8, 128), 0)
     gathered = a1[...]
-    at_end = jnp.where(r == GROUPS - 1, 0.0, 1.0)
+    counted = jnp.where(has_across, 1.0, 0.0)
     nxt = []
     for c in range(2):
         own_c = jnp.concatenate([gathered[k, 1 + c : 2 + c, :] for k in range(SLABS)], axis=0)
-        nxt.append(jnp.where(row8 == 7, nb[1 + c : 2 + c, :] * at_end, columns_back(own_c)))
+        outer = jnp.where(opposite, gathered[0, 1 + c : 2 + c, :], nb[1 + c : 2 + c, :]) * counted
+        nxt.append(jnp.where(row8 == 7, outer, columns_back(own_c)))
     zero8 = jnp.zeros((8, 128), F32)
     keep_parts([zero8, zero8] + nxt, 8)
     for p in range(4):
-        labels[p, 0:8, :] = jnp.concatenate([gathered[k, 3 + p : 4 + p, :] for k in range(SLABS)], axis=0)
+        outer = jnp.where(opposite, nb[3 + p : 4 + p, :], gathered[SLABS - 1, 3 + p : 4 + p, :])
+        labels[p, 0:8, :] = jnp.concatenate(
+            [gathered[k, 3 + p : 4 + p, :] for k in range(SLABS - 1)] + [outer], axis=0
+        )
     a2src[...] = label_sums(8, False) + jnp.sum(gathered, axis=0)[0:1, :]
     a2[r] = a2src[...]
+    pl.semaphore_wait(relay.at[1], 3)
     for device in far:
         push(a2src, a2.at[r], 10, recv.at[3], device)
 
@@ -547,9 +601,18 @@
     for device in peers:
         push(c1src, c1.at[s], 11, recv.at[4], device)
 
-    for k, halo in enumerate((halo_u, halo_f, halo_a)):
-        drained(halo.at[0], halo_recv.at[k, 0])
-        drained(halo.at[1], halo_recv.at[k, 1])
+    for side, has_side in enumerate((has_left, has_right)):
+
+        @pl.when(has_side)
+        def _():
+            for k, (own_ref, halo) in enumerate(strip):
+                drained(halo.at[side], halo_recv.at[k, side])
+
+        @pl.when(jnp.logical_not(has_side))
+        def _():
+            for own_ref, halo in strip:
+                halo[side] = jnp.zeros(halo.shape[1:], halo.dtype)
+
     column = lax.broadcasted_iota(jnp.int32, (EXT, 128), 0) + ((r * SLABS + s) * BLOCK - 8)
     inside = (column >= 0) & (column < GROUPS * SLABS * BLOCK)
 
@@ -685,15 +748,23 @@
 
     drained(a1.at[pl.ds(0, SLABS - 1)], send.at[0])
 
-    @pl.when(s == 0)
-    def _():
-        drained(a1, send.at[1])
+    @pl.when(gives_back)
+    def _():
+        drained(a1.at[pl.ds(0, 6)], send.at[1])
+
+    @pl.when(gives_on)
+    def _():
+        drained(a1.at[pl.ds(0, 2)], send.at[1])
 
     drained(pf.at[0, pl.ds(0, 3)], send.at[2])
     drained(pf.at[0], send.at[3])
-    for k, halo in enumerate((halo_u, halo_f, halo_a)):
-        drained(halo.at[1], send.at[4 + 2 * k])
-        drained(halo.at[0], send.at[5 + 2 * k])
+    for side, has_side in enumerate((has_left, has_right)):
+
+        @pl.when(has_side)
+        def _():
+            for k, (own_ref, halo) in enumerate(strip):
+                drained(halo.at[side], send.at[4 + 2 * k + side])
+
     drained(a2.at[pl.ds(0, GROUPS - 1)], send.at[10])
     drained(c1.at[pl.ds(0, SLABS - 1)], send.at[11])
     drained(c2.at[pl.ds(0, GROUPS - 1)], send.at[12])
@@ -781,6 +852,7 @@
             pltpu.VMEM((6, HALF, GRID), F32),
             pltpu.VMEM((CG_STEPS + 1, 2, BLOCK, 128), F32),
             pltpu.VMEM((4, 9, EXT, 128), F32),
+            pltpu.SemaphoreType.REGULAR((2,)),
             pltpu.SemaphoreType.DMA((5,)),
             pltpu.SemaphoreType.DMA((15,)),
             pltpu.SemaphoreType.DMA((8,)),

time: 48.8 us -> 47.5 us (0.973)
  Pallas kernels: 48 us -> 46.7 us
    pallas_call x1, Pallas kernels: 47.3 us -> 46 us  [shards(): pl.pallas_call(kernel, out_shape=(jax.ShapeDtypeStruct((2, BLOCK, 128), F...]
where the time goes in v4:
time: 47.5 us; the launch traced here: 47.4 us
  Pallas kernels  46.7 us (98%)
  between operations  0.64 us (1%)
    pallas_call x1, Pallas kernels, shards(): pl.pallas_call(kernel, out_shape=(jax.ShapeDtypeStruct((2, BLOCK, 128), F...  46 us

profile of v4, /device:TPU:1, one launch (start us, length us, event | category | flops | bytes accessed | tf_op | source)
XLA Modules:
  0.0 47.4 jit_solution(17672630275028616050)
XLA Ops:
  0.6 46.0 %fe2_step.1 = (f32[2,32,128]{2,1,0:T(8,128)S(1)}, f32[32,256]{1,0:T(8,128)S(1)}, f32[32,256]{1,0:T(8,128)S(1)}, f32[32,256]{1,0:T(8,128)S(1)}, f32[12,32]{1,0:T(8,128)S(1)}) custom-call(f32[2,32,128]{2,1,0:T(8,128)} %disp_hbm.1, f32[2,32,128]{2,1,0:T(8,128)} %body_hbm.1, s32[4,32,128]{2,1,0:T(8,128)} %assign_hbm.1, s32[1,32,256]{2,1,0:T(8,128)} %phase_hbm.1, ...), custom_call_target="tpu_custom_call" | custom-call | tf_op jit(solution)/shard_map/fe2_step/pallas_call | solution.py:815
  46.7 0.7 %write_out.1 = (f32[2,32,128]{2,1,0:T(8,128)}, f32[1,3,32,256]{3,2,1,0:T(8,128)}, f32[12,32]{1,0:T(8,128)}) custom-call(f32[2,32,128]{2,1,0:T(8,128)S(1)} %get-tuple-element.8.one, f32[32,256]{1,0:T(8,128)S(1)} %get-tuple-element.9.two_a, f32[32,256]{1,0:T(8,128)S(1)} %get-tuple-element.10.two_b, f32[32,256]{1,0:T(8,128)S(1)} %get-tuple-element.11.two_c, ...), custom_call_target="tpu_custom_call" | custom-call | tf_op jit(solution)/shard_map/write_out/pallas_call | solution.py:795

commit v5 on v4

--- a/solution.py
+++ b/solution.py
@@ -333,28 +333,18 @@
     for device in peers:
         push(a1src, a1.at[s], 0, recv.at[0], device)
 
+    strip = ((disp, halo_u), (body, halo_f), (assign, halo_a))
+
+    def tell(k, devices):
+        for device in devices:
+            pl.semaphore_signal(relay.at[k], inc=1, device_id=device, device_id_type=MESH)
+
+    tell(0, [ring_z[2], ring_z[6]])
     sibling = (r, y * 2 + 1 - core)
     for k in range(1, 4):
         push(pf.at[core, y], pf.at[core, y], 2, gather_recv.at[y], (r, lax.rem(y + k, 4) * 2 + core))
     push(pf.at[core, y], pf.at[core, y], 3, recv.at[2], sibling)
 
-    strip = ((disp, halo_u), (body, halo_f), (assign, halo_a))
-
-    @pl.when(has_left)
-    def _():
-        for k, (own_ref, halo) in enumerate(strip):
-            push(own_ref.at[:, pl.ds(0, 8), :], halo.at[1], 4 + 2 * k, halo_recv.at[k, 1], left)
-
-    @pl.when(has_right)
-    def _():
-        for k, (own_ref, halo) in enumerate(strip):
-            push(own_ref.at[:, pl.ds(BLOCK - 8, 8), :], halo.at[0], 5 + 2 * k, halo_recv.at[k, 0], right)
-
-    def tell(k, devices):
-        for device in devices:
-            pl.semaphore_signal(relay.at[k], inc=1, device_id=device, device_id_type=MESH)
-
-    tell(0, [ring_z[2], ring_z[6]])
     def symbols(k, _):
         rows = pl.ds(pl.multiple_of(k * 32, 32), 32)
         row = lax.broadcasted_iota(jnp.int32, (32, GRID), 0) + k * 32
@@ -405,6 +395,16 @@
     pl.semaphore_wait(relay.at[1], 3)
     for device in far:
         push(a2src, a2.at[r], 10, recv.at[3], device)
+
+    @pl.when(has_left)
+    def _():
+        for k, (own_ref, halo) in enumerate(strip):
+            push(own_ref.at[:, pl.ds(0, 8), :], halo.at[1], 4 + 2 * k, halo_recv.at[k, 1], left)
+
+    @pl.when(has_right)
+    def _():
+        for k, (own_ref, halo) in enumerate(strip):
+            push(own_ref.at[:, pl.ds(BLOCK - 8, 8), :], halo.at[0], 5 + 2 * k, halo_recv.at[k, 0], right)
 
     def take_block(slab, chip):
         rows = pl.ds(pl.multiple_of((chip * 2 + slab) * BLOCK, BLOCK), BLOCK)

time: 47.5 us -> 47.4 us (level)
  no operation moved by 1% of the time
where the time goes in v5:
time: 47.4 us; the launch traced here: 47.3 us
  Pallas kernels  46.7 us (99%)
  between operations  0.64 us (1%)
    pallas_call x1, Pallas kernels, shards(): pl.pallas_call(kernel, out_shape=(jax.ShapeDtypeStruct((2, BLOCK, 128), F...  46 us

profile of v5, /device:TPU:1, one launch (start us, length us, event | category | flops | bytes accessed | tf_op | source)
XLA Modules:
  0.0 47.3 jit_solution(7688868339699648041)
XLA Ops:
  0.6 46.0 %fe2_step.1 = (f32[2,32,128]{2,1,0:T(8,128)S(1)}, f32[32,256]{1,0:T(8,128)S(1)}, f32[32,256]{1,0:T(8,128)S(1)}, f32[32,256]{1,0:T(8,128)S(1)}, f32[12,32]{1,0:T(8,128)S(1)}) custom-call(f32[2,32,128]{2,1,0:T(8,128)} %disp_hbm.1, f32[2,32,128]{2,1,0:T(8,128)} %body_hbm.1, s32[4,32,128]{2,1,0:T(8,128)} %assign_hbm.1, s32[1,32,256]{2,1,0:T(8,128)} %phase_hbm.1, ...), custom_call_target="tpu_custom_call" | custom-call | tf_op jit(solution)/shard_map/fe2_step/pallas_call | solution.py:815
  46.6 0.7 %write_out.1 = (f32[2,32,128]{2,1,0:T(8,128)}, f32[1,3,32,256]{3,2,1,0:T(8,128)}, f32[12,32]{1,0:T(8,128)}) custom-call(f32[2,32,128]{2,1,0:T(8,128)S(1)} %get-tuple-element.8.one, f32[32,256]{1,0:T(8,128)S(1)} %get-tuple-element.9.two_a, f32[32,256]{1,0:T(8,128)S(1)} %get-tuple-element.10.two_b, f32[32,256]{1,0:T(8,128)S(1)} %get-tuple-element.11.two_c, ...), custom_call_target="tpu_custom_call" | custom-call | tf_op jit(solution)/shard_map/write_out/pallas_call | solution.py:795
